TPU v7x, 32 devices: a whole 2x2x4 slice. The times are simulated.
32 devices in a mesh: section: 4 (over y, x), fsdp: 8 (over z, core).
Axes of the slice: x: 2, y: 2, z: 4, core: 2. Of those that a mesh axis runs over, the one named last changes fastest.
Arguments:
- inputs: bfloat16 [4, 8, 256, 4096], P('section', None, 'fsdp'), may hold values from -6 to 6
- upstream: bfloat16 [8, 256, 4096], P(None, 'fsdp'), may hold values from -6 to 6
- weights: bfloat16 [4, 4096, 512], P('section', 'fsdp')
- gain: bfloat16 [4, 4096], P('section', 'fsdp'), may hold values from 0.5 to 1.5
Outputs:
- weight_grad: float32 [4, 4096, 512], P('section', 'fsdp')
- gain_grad: float32 [4, 4096], P('section')
All inputs are finite; a program needn't handle non-finite values.
Results may differ from a plain program's by a relative error of at most 0.035.
Values may be sent and summed in bfloat16 or wider, within the bound.
A program may use at most 128 MiB of HBM per device.

v0:
```python
import jax
import jax.numpy as jnp
from jax import lax
from jax.sharding import PartitionSpec as P


def passed_along(value, axis, steps):
    count = lax.axis_size(axis)
    leading, last = (max(0, -steps), min(count, count - steps))
    return lax.ppermute(value, axis, [(source, source + steps) for source in range(leading, last)])


def rope_tables(length, head):
    half_head = head // 2
    position = lax.iota(jnp.float32, length)
    freq = jnp.power(500000.0, -2.0 * lax.iota(jnp.float32, half_head) / head)
    angle = position[:, None] * freq[None, :]
    return (jnp.cos(angle), jnp.sin(angle))


def rotate(value_rows, cosine, sine_table):
    half_head = value_rows.shape[-1] // 2
    first = value_rows[..., :half_head]
    second = value_rows[..., half_head:]
    return jnp.concatenate(
        [first * cosine - second * sine_table, second * cosine + first * sine_table], axis=-1
    )


def unrotate(value_rows, cosine, sine_table):
    half_head = value_rows.shape[-1] // 2
    first = value_rows[..., :half_head]
    second = value_rows[..., half_head:]
    return jnp.concatenate(
        [first * cosine + second * sine_table, second * cosine - first * sine_table], axis=-1
    )


def contract_rows(left, right):
    return lax.dot_general(
        left, right, (((0,), (0,)), ((), ())), preferred_element_type=jnp.float32
    )


def contract_cols(left, right):
    return lax.dot_general(
        left, right, (((1,), (1,)), ((), ())), preferred_element_type=jnp.float32
    )


def on_device(inputs, upstream, weights, gain):
    sections = lax.axis_size("section")
    here = lax.axis_index("section")
    micro_count = inputs.shape[1]
    length = inputs.shape[2]
    width = inputs.shape[3]
    head = weights.shape[2] // 4
    tokens_all = micro_count * length
    xfloat = inputs[0].reshape(tokens_all, width).astype(jnp.float32)
    inv_rms = lax.rsqrt(jnp.mean(xfloat * xfloat, axis=1, keepdims=True) + 1e-05)
    normed = xfloat * inv_rms
    w_full, gain_full = (
        lax.all_gather(weights[0], "fsdp", axis=0, tiled=True),
        lax.all_gather(gain[0], "fsdp", axis=0, tiled=True),
    )
    hidden = (normed * gain_full.astype(jnp.float32)).astype(jnp.bfloat16)
    proj = jnp.dot(hidden, w_full[:, : 3 * head], preferred_element_type=jnp.float32)
    wide_gain = gain_full.astype(jnp.float32)
    w_proj = w_full[:, : 3 * head]
    w_back = w_full[:, 3 * head :]
    cosine, sine_table = rope_tables(length, head)
    proj_seq = proj.reshape(micro_count, length, 3 * head)
    query_rows = rotate(proj_seq[..., :head], cosine, sine_table).astype(jnp.bfloat16)
    key_rows = rotate(proj_seq[..., head : 2 * head], cosine, sine_table).astype(jnp.bfloat16)
    value_rows = proj_seq[..., 2 * head :].astype(jnp.bfloat16)
    score_scale = head ** (-0.5)
    causal = lax.broadcasted_iota(jnp.int32, (length, length), 0) >= lax.broadcasted_iota(
        jnp.int32, (length, length), 1
    )

    def work(micro, grad_in, state):
        grad_store, proj_store, att_store, gain_acc, extra = state
        query_m = lax.dynamic_index_in_dim(query_rows, micro, 0, keepdims=False)
        keys_m = lax.dynamic_index_in_dim(key_rows, micro, 0, keepdims=False)
        values_m = lax.dynamic_index_in_dim(value_rows, micro, 0, keepdims=False)
        normed_m = lax.dynamic_slice_in_dim(normed, micro * length, length, 0)
        inv_m = lax.dynamic_slice_in_dim(inv_rms, micro * length, length, 0)
        score_matrix = contract_cols(query_m, keys_m) * score_scale
        probs = jax.nn.softmax(jnp.where(causal, score_matrix, -1e30), axis=-1)
        probability_matrix = probs.astype(jnp.bfloat16)
        attended_output = jnp.dot(
            probability_matrix, values_m, preferred_element_type=jnp.float32
        ).astype(jnp.bfloat16)
        attention_gradient = jnp.dot(grad_in, w_back, preferred_element_type=jnp.float32).astype(
            jnp.bfloat16
        )
        probability_gradient = contract_cols(attention_gradient, values_m)
        score_gradient = (
            probs
            * (probability_gradient - jnp.sum(probability_gradient * probs, axis=-1, keepdims=True))
            * score_scale
        ).astype(jnp.bfloat16)
        query_gradient = jnp.dot(score_gradient, keys_m, preferred_element_type=jnp.float32)
        key_gradient = contract_rows(score_gradient, query_m)
        value_gradient = contract_rows(probability_matrix, attention_gradient)
        grad_proj = jnp.concatenate(
            [
                unrotate(query_gradient, cosine, sine_table),
                unrotate(key_gradient, cosine, sine_table),
                value_gradient,
            ],
            axis=-1,
        ).astype(jnp.bfloat16)
        grad_hidden = contract_cols(grad_proj, w_proj)
        gain_term = jnp.sum(grad_hidden * normed_m, axis=0)
        grad_normed = grad_hidden * wide_gain
        grad_x = inv_m * (
            grad_normed - normed_m * jnp.mean(grad_normed * normed_m, axis=-1, keepdims=True)
        )
        grad_out = (grad_in.astype(jnp.float32) + grad_x).astype(jnp.bfloat16)
        grad_store = lax.dynamic_update_index_in_dim(grad_store, grad_in, micro, 0)
        proj_store = lax.dynamic_update_index_in_dim(proj_store, grad_proj, micro, 0)
        att_store = lax.dynamic_update_index_in_dim(att_store, attended_output, micro, 0)
        return (grad_out, (grad_store, proj_store, att_store, gain_acc + gain_term, extra))

    def spare(micro, grad_in, state):
        return (jnp.zeros_like(grad_in), state)

    def tick(tick_no, received, state):
        micro = tick_no - (sections - 1 - here)
        active = jnp.logical_and(micro >= 0, micro < micro_count)
        clipped = jnp.clip(micro, 0, micro_count - 1)
        top_grad = lax.dynamic_index_in_dim(upstream, clipped, 0, keepdims=False)
        grad_in = jnp.where(here == sections - 1, top_grad, received)
        return lax.cond(active, work, spare, clipped, grad_in, state)

    def step_loop(tick_no, carry):
        received, state = carry
        sent, state = tick(tick_no, received, state)
        received = passed_along(sent, "section", -1)
        return (received, state)

    extra_start = jnp.zeros((1,), jnp.float32)
    state_start = (
        jnp.zeros((micro_count, length, width), jnp.bfloat16),
        jnp.zeros((micro_count, length, 3 * head), jnp.bfloat16),
        jnp.zeros((micro_count, length, head), jnp.bfloat16),
        jnp.zeros((width,), jnp.float32),
        extra_start,
    )
    total_ticks = sections + micro_count - 1
    received, state = lax.fori_loop(
        0, total_ticks - 1, step_loop, (jnp.zeros((length, width), jnp.bfloat16), state_start)
    )
    leftover, state = tick(total_ticks - 1, received, state)
    grad_store, proj_store, att_store, gain_acc, extra = state
    gain_sum = lax.psum(gain_acc, "fsdp")
    grad_flat = grad_store.reshape(tokens_all, width)
    proj_flat = proj_store.reshape(tokens_all, 3 * head)
    att_flat = att_store.reshape(tokens_all, head)
    shard = lax.psum_scatter(
        jnp.concatenate(
            [contract_rows(hidden, proj_flat), contract_rows(grad_flat, att_flat)], axis=1
        ).astype(jnp.bfloat16),
        "fsdp",
        scatter_dimension=0,
        tiled=True,
    ).astype(jnp.float32)
    return (shard[None], gain_sum[None])


def solution(mesh):
    return jax.shard_map(
        on_device,
        mesh=mesh,
        in_specs=(
            P("section", None, "fsdp", None),
            P(None, "fsdp", None),
            P("section", "fsdp", None),
            P("section", "fsdp"),
        ),
        out_specs=(P("section", "fsdp", None), P("section", None)),
        check_vma=False,
    )
```

profile of v0, /device:TPU:2, one launch (start us, length us, event | category | flops | bytes accessed | tf_op | source)
XLA Modules:
  0.0 381.2 jit_solution(9347632937482744176)
XLA Ops:
  8.0 2.1 multiply_reduce_fusion.4
  10.7 13.2 %all-gather = bf16[1,4096]{1,0:T(2,128)(2,1)S(1)} all-gather(bf16[1,512]{1,0:T(2,128)(2,1)} %param.13), channel_id=2, replica_groups=mesh['section'=4,'fsdp'=8] {'fsdp'}, dimensions={1}, use_global_device_ids=true | all-gather | bytes 9216 | tf_op jit(solution)/shard_map/all_gather | solution.py:64
  24.1 2.0 multiply_convert_fusion.2
  26.1 2.5 bitcast_multiply_fusion
  28.5 29.5 %all-gather.4.cloned.1.call-done = bf16[1,4096,512]{2,1,0:T(8,128)(2,1)} async-done(((bf16[1,512,512]{2,1,0:T(8,128)(2,1)}), bf16[1,4096,512]{2,1,0:T(8,128)(2,1)}) %all-gather.4.cloned.1.call-update) | async-done | bytes 4194320 | tf_op jit(solution)/shard_map/all_gather | solution.py:63
  58.0 3.3 fusion.70
  64.4 1.6 broadcast_in_dim.83
  68.0 238.8 %while.26 = (s32[]{:T(128)}, bf16[32,4096]{1,0:T(8,128)(2,1)}, bf16[8,32,4096]{2,1,0:T(8,128)(2,1)}, bf16[8,32,384]{2,1,0:T(8,128)(2,1)}, bf16[8,32,128]{2,1,0:T...) while((s32[]{:T(128)}, bf16[32,4096]{1,0:T(8,128)(2,1)}, ...), condition=%wide.region_9.10_spmd.clone.clone.clone, body=%wide.region_1.9_spmd.clone.clone.clone.sunk | while | flops 137564064 | bytes 10755985 | solution.py:152
  68.8 2.5 collective-permute-start
  71.3 9.0 %collective-permute-done = bf16[32,4096]{1,0:T(8,128)(2,1)S(1)} collective-permute-done((bf16[32,4096]{1,0:T(8,128)(2,1)}, bf16[32,4096]{1,0:T(8,128)(2,1)S(1)}, u32[]{:S(2)}, u32[]{:S(2)}) %collective-permute-start) | collective-permute-done | bytes 262176 | tf_op jit(solution)/shard_map/while/body/eval_jaxpr/ppermute | solution.py:10
  81.7 1.9 collective-permute-start
  83.6 31.6 %collective-permute-done = bf16[32,4096]{1,0:T(8,128)(2,1)S(1)} collective-permute-done((bf16[32,4096]{1,0:T(8,128)(2,1)}, bf16[32,4096]{1,0:T(8,128)(2,1)S(1)}, u32[]{:S(2)}, u32[]{:S(2)}) %collective-permute-start) | collective-permute-done | bytes 262176 | tf_op jit(solution)/shard_map/while/body/eval_jaxpr/ppermute | solution.py:10
  116.0 13.6 %conditional.7 = (bf16[32,4096]{1,0:T(8,128)(2,1)}, bf16[8,32,4096]{2,1,0:T(8,128)(2,1)}, bf16[8,32,384]{2,1,0:T(8,128)(2,1)}, bf16[8,32,128]{2,1,0:T(8,128)(2,1)}, f32[4096]{0:T(1024)S(1)}) conditional(s32[]{:T(128)} %convert_element_type.189, (bf16[8,32,4096]{2,1,0:T(8,128)(2,1)}, bf16[8,32,384]{2,1,0:T(8,128)(2,1)}, ...), branch_computations={%region_2.2_spmd, %region_3.8_spmd.clone} | conditional | flops 137562016 | bytes 8641706 | solution.py:135
  117.0 1.8 bitcast_dynamic-update-slice_fusion.1
  123.9 2.2 multiply_reduce_fusion.1
  126.2 1.9 add_convert_fusion.2
  129.6 1.9 collective-permute-start
  131.5 8.4 %collective-permute-done = bf16[32,4096]{1,0:T(8,128)(2,1)S(1)} collective-permute-done((bf16[32,4096]{1,0:T(8,128)(2,1)}, bf16[32,4096]{1,0:T(8,128)(2,1)S(1)}, u32[]{:S(2)}, u32[]{:S(2)}) %collective-permute-start) | collective-permute-done | bytes 262176 | tf_op jit(solution)/shard_map/while/body/eval_jaxpr/ppermute | solution.py:10
  140.7 13.6 %conditional.7 = (bf16[32,4096]{1,0:T(8,128)(2,1)}, bf16[8,32,4096]{2,1,0:T(8,128)(2,1)}, bf16[8,32,384]{2,1,0:T(8,128)(2,1)}, bf16[8,32,128]{2,1,0:T(8,128)(2,1)}, f32[4096]{0:T(1024)S(1)}) conditional(s32[]{:T(128)} %convert_element_type.189, (bf16[8,32,4096]{2,1,0:T(8,128)(2,1)}, bf16[8,32,384]{2,1,0:T(8,128)(2,1)}, ...), branch_computations={%region_2.2_spmd, %region_3.8_spmd.clone} | conditional | flops 137562016 | bytes 8641706 | solution.py:135
  141.7 1.8 bitcast_dynamic-update-slice_fusion.1
  148.6 2.2 multiply_reduce_fusion.1
  150.9 1.9 add_convert_fusion.2
  154.3 1.9 collective-permute-start
  156.3 7.5 %collective-permute-done = bf16[32,4096]{1,0:T(8,128)(2,1)S(1)} collective-permute-done((bf16[32,4096]{1,0:T(8,128)(2,1)}, bf16[32,4096]{1,0:T(8,128)(2,1)S(1)}, u32[]{:S(2)}, u32[]{:S(2)}) %collective-permute-start) | collective-permute-done | bytes 262176 | tf_op jit(solution)/shard_map/while/body/eval_jaxpr/ppermute | solution.py:10
  164.5 13.6 %conditional.7 = (bf16[32,4096]{1,0:T(8,128)(2,1)}, bf16[8,32,4096]{2,1,0:T(8,128)(2,1)}, bf16[8,32,384]{2,1,0:T(8,128)(2,1)}, bf16[8,32,128]{2,1,0:T(8,128)(2,1)}, f32[4096]{0:T(1024)S(1)}) conditional(s32[]{:T(128)} %convert_element_type.189, (bf16[8,32,4096]{2,1,0:T(8,128)(2,1)}, bf16[8,32,384]{2,1,0:T(8,128)(2,1)}, ...), branch_computations={%region_2.2_spmd, %region_3.8_spmd.clone} | conditional | flops 137562016 | bytes 8641706 | solution.py:135
  165.5 1.8 bitcast_dynamic-update-slice_fusion.1
  172.4 2.2 multiply_reduce_fusion.1
  174.7 1.9 add_convert_fusion.2
  178.1 1.9 collective-permute-start
  180.1 7.4 %collective-permute-done = bf16[32,4096]{1,0:T(8,128)(2,1)S(1)} collective-permute-done((bf16[32,4096]{1,0:T(8,128)(2,1)}, bf16[32,4096]{1,0:T(8,128)(2,1)S(1)}, u32[]{:S(2)}, u32[]{:S(2)}) %collective-permute-start) | collective-permute-done | bytes 262176 | tf_op jit(solution)/shard_map/while/body/eval_jaxpr/ppermute | solution.py:10
  188.3 13.6 %conditional.7 = (bf16[32,4096]{1,0:T(8,128)(2,1)}, bf16[8,32,4096]{2,1,0:T(8,128)(2,1)}, bf16[8,32,384]{2,1,0:T(8,128)(2,1)}, bf16[8,32,128]{2,1,0:T(8,128)(2,1)}, f32[4096]{0:T(1024)S(1)}) conditional(s32[]{:T(128)} %convert_element_type.189, (bf16[8,32,4096]{2,1,0:T(8,128)(2,1)}, bf16[8,32,384]{2,1,0:T(8,128)(2,1)}, ...), branch_computations={%region_2.2_spmd, %region_3.8_spmd.clone} | conditional | flops 137562016 | bytes 8641706 | solution.py:135
  189.2 1.8 bitcast_dynamic-update-slice_fusion.1
  196.1 2.2 multiply_reduce_fusion.1
  198.5 1.9 add_convert_fusion.2
  201.9 1.9 collective-permute-start
  203.8 7.4 %collective-permute-done = bf16[32,4096]{1,0:T(8,128)(2,1)S(1)} collective-permute-done((bf16[32,4096]{1,0:T(8,128)(2,1)}, bf16[32,4096]{1,0:T(8,128)(2,1)S(1)}, u32[]{:S(2)}, u32[]{:S(2)}) %collective-permute-start) | collective-permute-done | bytes 262176 | tf_op jit(solution)/shard_map/while/body/eval_jaxpr/ppermute | solution.py:10
  212.0 13.6 %conditional.7 = (bf16[32,4096]{1,0:T(8,128)(2,1)}, bf16[8,32,4096]{2,1,0:T(8,128)(2,1)}, bf16[8,32,384]{2,1,0:T(8,128)(2,1)}, bf16[8,32,128]{2,1,0:T(8,128)(2,1)}, f32[4096]{0:T(1024)S(1)}) conditional(s32[]{:T(128)} %convert_element_type.189, (bf16[8,32,4096]{2,1,0:T(8,128)(2,1)}, bf16[8,32,384]{2,1,0:T(8,128)(2,1)}, ...), branch_computations={%region_2.2_spmd, %region_3.8_spmd.clone} | conditional | flops 137562016 | bytes 8641706 | solution.py:135
  212.9 1.8 bitcast_dynamic-update-slice_fusion.1
  219.9 2.2 multiply_reduce_fusion.1
  222.2 1.9 add_convert_fusion.2
  225.6 1.9 collective-permute-start
  227.5 7.4 %collective-permute-done = bf16[32,4096]{1,0:T(8,128)(2,1)S(1)} collective-permute-done((bf16[32,4096]{1,0:T(8,128)(2,1)}, bf16[32,4096]{1,0:T(8,128)(2,1)S(1)}, u32[]{:S(2)}, u32[]{:S(2)}) %collective-permute-start) | collective-permute-done | bytes 262176 | tf_op jit(solution)/shard_map/while/body/eval_jaxpr/ppermute | solution.py:10
  235.7 13.6 %conditional.7 = (bf16[32,4096]{1,0:T(8,128)(2,1)}, bf16[8,32,4096]{2,1,0:T(8,128)(2,1)}, bf16[8,32,384]{2,1,0:T(8,128)(2,1)}, bf16[8,32,128]{2,1,0:T(8,128)(2,1)}, f32[4096]{0:T(1024)S(1)}) conditional(s32[]{:T(128)} %convert_element_type.189, (bf16[8,32,4096]{2,1,0:T(8,128)(2,1)}, bf16[8,32,384]{2,1,0:T(8,128)(2,1)}, ...), branch_computations={%region_2.2_spmd, %region_3.8_spmd.clone} | conditional | flops 137562016 | bytes 8641706 | solution.py:135
  236.6 1.8 bitcast_dynamic-update-slice_fusion.1
  243.6 2.2 multiply_reduce_fusion.1
  245.9 1.9 add_convert_fusion.2
  249.3 1.9 collective-permute-start
  251.2 7.4 %collective-permute-done = bf16[32,4096]{1,0:T(8,128)(2,1)S(1)} collective-permute-done((bf16[32,4096]{1,0:T(8,128)(2,1)}, bf16[32,4096]{1,0:T(8,128)(2,1)S(1)}, u32[]{:S(2)}, u32[]{:S(2)}) %collective-permute-start) | collective-permute-done | bytes 262176 | tf_op jit(solution)/shard_map/while/body/eval_jaxpr/ppermute | solution.py:10
  259.4 13.6 %conditional.7 = (bf16[32,4096]{1,0:T(8,128)(2,1)}, bf16[8,32,4096]{2,1,0:T(8,128)(2,1)}, bf16[8,32,384]{2,1,0:T(8,128)(2,1)}, bf16[8,32,128]{2,1,0:T(8,128)(2,1)}, f32[4096]{0:T(1024)S(1)}) conditional(s32[]{:T(128)} %convert_element_type.189, (bf16[8,32,4096]{2,1,0:T(8,128)(2,1)}, bf16[8,32,384]{2,1,0:T(8,128)(2,1)}, ...), branch_computations={%region_2.2_spmd, %region_3.8_spmd.clone} | conditional | flops 137562016 | bytes 8641706 | solution.py:135
  260.4 1.8 bitcast_dynamic-update-slice_fusion.1
  267.3 2.2 multiply_reduce_fusion.1
  269.7 1.9 add_convert_fusion.2
  273.0 1.9 collective-permute-start
  275.0 7.4 %collective-permute-done = bf16[32,4096]{1,0:T(8,128)(2,1)S(1)} collective-permute-done((bf16[32,4096]{1,0:T(8,128)(2,1)}, bf16[32,4096]{1,0:T(8,128)(2,1)S(1)}, u32[]{:S(2)}, u32[]{:S(2)}) %collective-permute-start) | collective-permute-done | bytes 262176 | tf_op jit(solution)/shard_map/while/body/eval_jaxpr/ppermute | solution.py:10
  283.2 13.6 %conditional.7 = (bf16[32,4096]{1,0:T(8,128)(2,1)}, bf16[8,32,4096]{2,1,0:T(8,128)(2,1)}, bf16[8,32,384]{2,1,0:T(8,128)(2,1)}, bf16[8,32,128]{2,1,0:T(8,128)(2,1)}, f32[4096]{0:T(1024)S(1)}) conditional(s32[]{:T(128)} %convert_element_type.189, (bf16[8,32,4096]{2,1,0:T(8,128)(2,1)}, bf16[8,32,384]{2,1,0:T(8,128)(2,1)}, ...), branch_computations={%region_2.2_spmd, %region_3.8_spmd.clone} | conditional | flops 137562016 | bytes 8641706 | solution.py:135
  284.1 1.8 bitcast_dynamic-update-slice_fusion.1
  291.0 2.2 multiply_reduce_fusion.1
  293.4 1.9 add_convert_fusion.2
  296.8 1.9 collective-permute-start
  298.7 7.4 %collective-permute-done = bf16[32,4096]{1,0:T(8,128)(2,1)S(1)} collective-permute-done((bf16[32,4096]{1,0:T(8,128)(2,1)}, bf16[32,4096]{1,0:T(8,128)(2,1)S(1)}, u32[]{:S(2)}, u32[]{:S(2)}) %collective-permute-start) | collective-permute-done | bytes 262176 | tf_op jit(solution)/shard_map/while/body/eval_jaxpr/ppermute | solution.py:10
  306.9 2.8 convolution_convert_fusion.6
  311.0 2.3 pad_maximum_fusion
  313.3 27.0 %psum.7 = f32[1,4096]{1,0:T(1,128)} all-reduce(f32[1,4096]{1,0:T(1,128)S(1)} %bitcast.141), channel_id=1, replica_groups=mesh['section'=4,'fsdp'=8] {'fsdp'}, use_global_device_ids=true, to_apply=%region_17.18 | all-reduce | flops 4096 | bytes 32768 | tf_op jit(solution)/shard_map/psum | solution.py:157
  340.3 31.6 %reduce-scatter.2.cloned.1.call-done = bf16[512,512]{0,1:T(8,128)(2,1)} async-done(((bf16[4096,512]{0,1:T(8,128)(2,1)}), bf16[512,512]{0,1:T(8,128)(2,1)}) %reduce-scatter.2.cloned.1.call-update) | async-done | bytes 524304 | tf_op jit(solution)/shard_map/reduce_scatter | solution.py:161
  (233 shorter events, 81.1 us)
Async XLA Ops:
  7.2 16.9 %copy-start = (bf16[1,8,32,4096]{3,2,1,0:T(8,128)(2,1)S(1)}, bf16[1,8,32,4096]{3,2,1,0:T(8,128)(2,1)}, u32[]{:S(2)}) copy-start(bf16[1,8,32,4096]{3,2,1,0:T(8,128)(2,1)} %param.10) | copy-start | bytes 6291460
  7.2 50.9 %all-gather.4.cloned.1.call-start = ((), (), s32[]{:S(2)}) async-start(), calls=%async_computation.2 | async-start | bytes 4718592 | tf_op jit(solution)/shard_map/all_gather | solution.py:63
  7.9 364.0 %reduce-scatter.2.cloned.1.call-start = ((), (), s32[]{:S(2)}) async-start(), calls=%async_computation.1 | async-start | bytes 4718592 | tf_op jit(solution)/shard_map/reduce_scatter | solution.py:161
  24.0 39.4 %copy-start.5 = (f32[32,64]{1,0:T(8,128)}, f32[32,64]{1,0:T(8,128)S(1)}, u32[]{:S(2)}) copy-start(f32[32,64]{1,0:T(8,128)S(1)} %get-tuple-element.1387) | copy-start | bytes 24580
  24.0 39.4 %copy-start.6 = (f32[32,64]{1,0:T(8,128)}, f32[32,64]{1,0:T(8,128)S(1)}, u32[]{:S(2)}) copy-start(f32[32,64]{1,0:T(8,128)S(1)} %get-tuple-element.1388) | copy-start | bytes 24580
  58.0 3.4 copy-start.4
  68.8 11.4 %collective-permute-start = (bf16[32,4096]{1,0:T(8,128)(2,1)}, bf16[32,4096]{1,0:T(8,128)(2,1)S(1)}, u32[]{:S(2)}, u32[]{:S(2)}) collective-permute-start(bf16[32,4096]{1,0:T(8,128)(2,1)} %get-tuple-element.1280), channel_id=1, source_target_pairs={{8,0},{16,8},{24,16},{9,1},{17,9},{25,17},{10,2},{18,10},{26,18},{... | collective-permute-start | bytes 786440 | tf_op jit(solution)/shard_map/while/body/eval_jaxpr/ppermute | solution.py:10
  80.2 0.7 copy-start.2
  81.7 33.6 %collective-permute-start = (bf16[32,4096]{1,0:T(8,128)(2,1)}, bf16[32,4096]{1,0:T(8,128)(2,1)S(1)}, u32[]{:S(2)}, u32[]{:S(2)}) collective-permute-start(bf16[32,4096]{1,0:T(8,128)(2,1)} %get-tuple-element.1280), channel_id=1, source_target_pairs={{8,0},{16,8},{24,16},{9,1},{17,9},{25,17},{10,2},{18,10},{26,18},{... | collective-permute-start | bytes 786440 | tf_op jit(solution)/shard_map/while/body/eval_jaxpr/ppermute | solution.py:10
  115.3 0.7 copy-start.2
  118.8 7.4 %copy-start.7 = (f32[256,1]{0,1:T(1,128)S(1)}, f32[256,1]{0,1:T(1,128)}, u32[]{:S(2)}) copy-start(f32[256,1]{0,1:T(1,128)} %get-tuple-element.1061) | copy-start | bytes 3076 | tf_op jit(solution)/shard_map/while/body/eval_jaxpr/cond
  129.6 10.4 %collective-permute-start = (bf16[32,4096]{1,0:T(8,128)(2,1)}, bf16[32,4096]{1,0:T(8,128)(2,1)S(1)}, u32[]{:S(2)}, u32[]{:S(2)}) collective-permute-start(bf16[32,4096]{1,0:T(8,128)(2,1)} %get-tuple-element.1280), channel_id=1, source_target_pairs={{8,0},{16,8},{24,16},{9,1},{17,9},{25,17},{10,2},{18,10},{26,18},{... | collective-permute-start | bytes 786440 | tf_op jit(solution)/shard_map/while/body/eval_jaxpr/ppermute | solution.py:10
  140.0 0.7 copy-start.2
  143.5 7.4 %copy-start.7 = (f32[256,1]{0,1:T(1,128)S(1)}, f32[256,1]{0,1:T(1,128)}, u32[]{:S(2)}) copy-start(f32[256,1]{0,1:T(1,128)} %get-tuple-element.1061) | copy-start | bytes 3076 | tf_op jit(solution)/shard_map/while/body/eval_jaxpr/cond
  154.3 9.4 %collective-permute-start = (bf16[32,4096]{1,0:T(8,128)(2,1)}, bf16[32,4096]{1,0:T(8,128)(2,1)S(1)}, u32[]{:S(2)}, u32[]{:S(2)}) collective-permute-start(bf16[32,4096]{1,0:T(8,128)(2,1)} %get-tuple-element.1280), channel_id=1, source_target_pairs={{8,0},{16,8},{24,16},{9,1},{17,9},{25,17},{10,2},{18,10},{26,18},{... | collective-permute-start | bytes 786440 | tf_op jit(solution)/shard_map/while/body/eval_jaxpr/ppermute | solution.py:10
  163.8 0.7 copy-start.2
  167.3 7.4 %copy-start.7 = (f32[256,1]{0,1:T(1,128)S(1)}, f32[256,1]{0,1:T(1,128)}, u32[]{:S(2)}) copy-start(f32[256,1]{0,1:T(1,128)} %get-tuple-element.1061) | copy-start | bytes 3076 | tf_op jit(solution)/shard_map/while/body/eval_jaxpr/cond
  178.1 9.4 %collective-permute-start = (bf16[32,4096]{1,0:T(8,128)(2,1)}, bf16[32,4096]{1,0:T(8,128)(2,1)S(1)}, u32[]{:S(2)}, u32[]{:S(2)}) collective-permute-start(bf16[32,4096]{1,0:T(8,128)(2,1)} %get-tuple-element.1280), channel_id=1, source_target_pairs={{8,0},{16,8},{24,16},{9,1},{17,9},{25,17},{10,2},{18,10},{26,18},{... | collective-permute-start | bytes 786440 | tf_op jit(solution)/shard_map/while/body/eval_jaxpr/ppermute | solution.py:10
  187.5 0.7 copy-start.2
  191.0 7.4 %copy-start.7 = (f32[256,1]{0,1:T(1,128)S(1)}, f32[256,1]{0,1:T(1,128)}, u32[]{:S(2)}) copy-start(f32[256,1]{0,1:T(1,128)} %get-tuple-element.1061) | copy-start | bytes 3076 | tf_op jit(solution)/shard_map/while/body/eval_jaxpr/cond
  201.9 9.4 %collective-permute-start = (bf16[32,4096]{1,0:T(8,128)(2,1)}, bf16[32,4096]{1,0:T(8,128)(2,1)S(1)}, u32[]{:S(2)}, u32[]{:S(2)}) collective-permute-start(bf16[32,4096]{1,0:T(8,128)(2,1)} %get-tuple-element.1280), channel_id=1, source_target_pairs={{8,0},{16,8},{24,16},{9,1},{17,9},{25,17},{10,2},{18,10},{26,18},{... | collective-permute-start | bytes 786440 | tf_op jit(solution)/shard_map/while/body/eval_jaxpr/ppermute | solution.py:10
  211.2 0.7 copy-start.2
  214.7 7.4 %copy-start.7 = (f32[256,1]{0,1:T(1,128)S(1)}, f32[256,1]{0,1:T(1,128)}, u32[]{:S(2)}) copy-start(f32[256,1]{0,1:T(1,128)} %get-tuple-element.1061) | copy-start | bytes 3076 | tf_op jit(solution)/shard_map/while/body/eval_jaxpr/cond
  225.6 9.4 %collective-permute-start = (bf16[32,4096]{1,0:T(8,128)(2,1)}, bf16[32,4096]{1,0:T(8,128)(2,1)S(1)}, u32[]{:S(2)}, u32[]{:S(2)}) collective-permute-start(bf16[32,4096]{1,0:T(8,128)(2,1)} %get-tuple-element.1280), channel_id=1, source_target_pairs={{8,0},{16,8},{24,16},{9,1},{17,9},{25,17},{10,2},{18,10},{26,18},{... | collective-permute-start | bytes 786440 | tf_op jit(solution)/shard_map/while/body/eval_jaxpr/ppermute | solution.py:10
  235.0 0.7 copy-start.2
  238.4 7.4 %copy-start.7 = (f32[256,1]{0,1:T(1,128)S(1)}, f32[256,1]{0,1:T(1,128)}, u32[]{:S(2)}) copy-start(f32[256,1]{0,1:T(1,128)} %get-tuple-element.1061) | copy-start | bytes 3076 | tf_op jit(solution)/shard_map/while/body/eval_jaxpr/cond
  249.3 9.4 %collective-permute-start = (bf16[32,4096]{1,0:T(8,128)(2,1)}, bf16[32,4096]{1,0:T(8,128)(2,1)S(1)}, u32[]{:S(2)}, u32[]{:S(2)}) collective-permute-start(bf16[32,4096]{1,0:T(8,128)(2,1)} %get-tuple-element.1280), channel_id=1, source_target_pairs={{8,0},{16,8},{24,16},{9,1},{17,9},{25,17},{10,2},{18,10},{26,18},{... | collective-permute-start | bytes 786440 | tf_op jit(solution)/shard_map/while/body/eval_jaxpr/ppermute | solution.py:10
  258.7 0.7 copy-start.2
  262.2 7.4 %copy-start.7 = (f32[256,1]{0,1:T(1,128)S(1)}, f32[256,1]{0,1:T(1,128)}, u32[]{:S(2)}) copy-start(f32[256,1]{0,1:T(1,128)} %get-tuple-element.1061) | copy-start | bytes 3076 | tf_op jit(solution)/shard_map/while/body/eval_jaxpr/cond
  273.0 9.4 %collective-permute-start = (bf16[32,4096]{1,0:T(8,128)(2,1)}, bf16[32,4096]{1,0:T(8,128)(2,1)S(1)}, u32[]{:S(2)}, u32[]{:S(2)}) collective-permute-start(bf16[32,4096]{1,0:T(8,128)(2,1)} %get-tuple-element.1280), channel_id=1, source_target_pairs={{8,0},{16,8},{24,16},{9,1},{17,9},{25,17},{10,2},{18,10},{26,18},{... | collective-permute-start | bytes 786440 | tf_op jit(solution)/shard_map/while/body/eval_jaxpr/ppermute | solution.py:10
  282.4 0.7 copy-start.2
  285.9 7.4 %copy-start.7 = (f32[256,1]{0,1:T(1,128)S(1)}, f32[256,1]{0,1:T(1,128)}, u32[]{:S(2)}) copy-start(f32[256,1]{0,1:T(1,128)} %get-tuple-element.1061) | copy-start | bytes 3076 | tf_op jit(solution)/shard_map/while/body/eval_jaxpr/cond
  296.8 9.4 %collective-permute-start = (bf16[32,4096]{1,0:T(8,128)(2,1)}, bf16[32,4096]{1,0:T(8,128)(2,1)S(1)}, u32[]{:S(2)}, u32[]{:S(2)}) collective-permute-start(bf16[32,4096]{1,0:T(8,128)(2,1)} %get-tuple-element.1280), channel_id=1, source_target_pairs={{8,0},{16,8},{24,16},{9,1},{17,9},{25,17},{10,2},{18,10},{26,18},{... | collective-permute-start | bytes 786440 | tf_op jit(solution)/shard_map/while/body/eval_jaxpr/ppermute | solution.py:10
  306.1 0.7 copy-start.2
  306.9 2.8 copy-start.1
Sparse Core Ops, SparseCore 0:
  9.6 48.3 all-gather.3
  313.5 58.3 reduce-scatter.1
where the time goes:
time: 386 us; the launch traced here: 381 us
  waiting for transfers between devices  163 us (42%)
  matrix products  77.2 us (20%)
  other arithmetic  42.5 us (11%)
  blocking collectives  40.1 us (10%)
  local copies, waits for them, and re-layouts  23.4 us (6%)
  starting transfers between devices  19.7 us (5%)
  between operations  14.2 us (4%)
    ppermute x10, waiting for transfers between devices, passed_along(): lax.ppermute(value, axis, [(source, source + steps) for source in range(l...  101 us
    reduce_scatter x1, waiting for transfers between devices, on_device(): lax.psum_scatter(jnp.concatenate([contract_rows(hidden, proj_flat), contr...  31.6 us
    dot_general x24, matrix products, contract_cols(): lax.dot_general(left, right, (((1,), (1,)), ((), ())), preferred_element_...  31.5 us
    all_gather x1, waiting for transfers between devices, on_device(): lax.all_gather(weights[0], 'fsdp', axis=0, tiled=True)  29.5 us
    psum x1, blocking collectives, on_device(): gain_sum = lax.psum(gain_acc, 'fsdp')  27 us
    ppermute x10, starting transfers between devices, passed_along(): lax.ppermute(value, axis, [(source, source + steps) for source in range(l...  19.6 us
    convert_element_type x8, other arithmetic, work(): grad_out = (grad_in.astype(jnp.float32) + grad_x).astype(jnp.bfloat16)  15.3 us
    dynamic_update_slice x8, other arithmetic, work(): grad_store = lax.dynamic_update_index_in_dim(grad_store, grad_in, micro, 0)  14.5 us
  transfers between devices with their start and end apart: 12, of which 12 were waited for; matrix products, arithmetic and copies ran while one was open for 2% of the time, Pallas kernels for 0%

commit v1 on v0

v1 whole, which is shorter than its diff:
```python
import jax
import jax.numpy as jnp
from jax import lax
from jax.sharding import PartitionSpec as P

F32 = jnp.float32
BF16 = jnp.bfloat16


def rope_tables(length, head):
    half_head = head // 2
    position = lax.iota(F32, length)
    freq = jnp.power(500000.0, -2.0 * lax.iota(F32, half_head) / head)
    angle = position[:, None] * freq[None, :]
    return (jnp.cos(angle), jnp.sin(angle))


def turn(rows, cos_full, sin_full):
    half = rows.shape[-1] // 2
    swapped = jnp.concatenate([rows[:, half:], rows[:, :half]], axis=-1)
    return rows * cos_full + swapped * sin_full


def dot(left, right):
    return jnp.dot(left, right, preferred_element_type=F32)


def dot_rows(left, right):
    return lax.dot_general(left, right, (((0,), (0,)), ((), ())), preferred_element_type=F32)


def dot_cols(left, right):
    return lax.dot_general(left, right, (((1,), (1,)), ((), ())), preferred_element_type=F32)


def on_device(inputs, upstream, weights, gain):
    sections = lax.axis_size("section")
    here = lax.axis_index("section")
    micro_count, length, width = inputs.shape[1:]
    head = weights.shape[2] // 4
    tokens = micro_count * length
    lower = sections - 1
    x = inputs[0].reshape(tokens, width)
    up = upstream.reshape(tokens, width)
    w_own = weights[0].astype(F32)
    gain_own = gain[0].astype(F32)[:, None]
    w_scaled = (w_own[:, : 3 * head] * gain_own).astype(BF16)
    w_back_own = weights[0][:, 3 * head :]

    w_full = lax.all_gather(
        jnp.concatenate([w_scaled, w_back_own], axis=1), "fsdp", axis=0, tiled=True
    )
    backs = lax.all_gather(w_back_own, "section", axis=0)[:lower]
    backs = jnp.transpose(backs, (1, 0, 2)).reshape(w_back_own.shape[0], lower * head)
    back_all = lax.all_gather(backs, "fsdp", axis=0, tiled=True)
    wg = w_full[:, : 3 * head]
    wb = w_full[:, 3 * head :]

    xfloat = x.astype(F32)
    inv = lax.rsqrt(jnp.mean(xfloat * xfloat, axis=1, keepdims=True) + 1e-05)
    proj = dot(x, wg) * inv
    direct = dot(up, wb)

    cosine, sine = rope_tables(length, head)
    cos_full = jnp.tile(jnp.concatenate([cosine, cosine], axis=1), (micro_count, 1))
    sin_full = jnp.tile(jnp.concatenate([-sine, sine], axis=1), (micro_count, 1))
    query = turn(proj[:, :head], cos_full, sin_full).astype(BF16)
    keys = turn(proj[:, head : 2 * head], cos_full, sin_full).astype(BF16)
    values = proj[:, 2 * head :].astype(BF16)
    scale = head ** (-0.5)
    row = lax.broadcasted_iota(jnp.int32, (tokens, tokens), 0)
    col = lax.broadcasted_iota(jnp.int32, (tokens, tokens), 1)
    seen = jnp.logical_and(row // length == col // length, row >= col)
    scores = jnp.where(seen, dot_cols(query, keys) * scale, -1e30)
    peak = jnp.max(scores, axis=1, keepdims=True)
    expd = jnp.where(seen, jnp.exp(scores - peak), 0.0)
    probs = expd / jnp.sum(expd, axis=1, keepdims=True)
    probs_b = probs.astype(BF16)
    attended = dot(probs_b, values).astype(BF16)
    att_all = lax.all_gather(attended, "section", axis=0)[:lower]
    att_all = jnp.transpose(att_all, (1, 0, 2)).reshape(tokens, lower * head)

    cross = dot_rows(wg, back_all).astype(BF16)
    through = dot(x, back_all) * inv

    def backward(grad_att):
        grad_att = grad_att.astype(BF16)
        grad_probs = dot_cols(grad_att, values)
        grad_scores = (
            probs
            * (grad_probs - jnp.sum(grad_probs * probs, axis=1, keepdims=True))
            * scale
        ).astype(BF16)
        return jnp.concatenate(
            [
                turn(dot(grad_scores, keys), cos_full, -sin_full),
                turn(dot_rows(grad_scores, query), cos_full, -sin_full),
                dot_rows(probs_b, grad_att),
            ],
            axis=1,
        ).astype(BF16)

    received = jnp.zeros((tokens, lower * head), BF16)
    own_at = jnp.minimum(here, lower - 1) * head
    for tick in range(sections):
        own = lax.dynamic_slice_in_dim(received, own_at, head, 1).astype(F32)
        own = jnp.where(here == sections - 1, 0.0, own)
        grad_proj = backward(direct + own)
        shift = jnp.sum(grad_proj.astype(F32) * proj, axis=1, keepdims=True) / width
        if tick < sections - 1:
            sent = received.astype(F32) + inv * (dot(grad_proj, cross) - shift * through)
            received = lax.ppermute(
                sent.astype(BF16), "section", [(s, s - 1) for s in range(1, sections)]
            )

    below = lax.iota(jnp.int32, lower * head)[None, :] < here * head
    att_below = jnp.where(below, att_all, jnp.zeros((), BF16))
    scaled_proj = (grad_proj.astype(F32) * inv).astype(BF16)
    scaled_att = (att_below.astype(F32) * (inv * inv * shift)).astype(BF16)
    by_x = dot_rows(x, jnp.concatenate([scaled_proj, scaled_att], axis=1))
    mixed = dot_rows(scaled_proj, att_below).astype(BF16)
    term = jnp.concatenate(
        [
            by_x[:, : 3 * head],
            dot_rows(up, attended),
            dot(wg, mixed) - by_x[:, 3 * head :],
        ],
        axis=1,
    ).astype(BF16)
    total = lax.psum_scatter(term, "fsdp", scatter_dimension=0, tiled=True)
    rows = total.shape[0]
    handed = total[:, 4 * head :].reshape(rows, lower, head)
    handed = jnp.concatenate([handed, jnp.zeros((rows, 1, head), BF16)], axis=1)
    handed = lax.psum_scatter(
        jnp.transpose(handed, (1, 0, 2)), "section", scatter_dimension=0, tiled=False
    )
    raw = total[:, : 3 * head].astype(F32)
    shard = jnp.concatenate(
        [raw * gain_own, total[:, 3 * head : 4 * head].astype(F32) + handed.astype(F32)], axis=1
    )
    gain_rows = jnp.sum(raw * w_own[:, : 3 * head], axis=1)
    gain_sum = lax.all_gather(gain_rows, "fsdp", axis=0, tiled=True)
    return (shard[None], gain_sum[None])


def solution(mesh):
    return jax.shard_map(
        on_device,
        mesh=mesh,
        in_specs=(
            P("section", None, "fsdp", None),
            P(None, "fsdp", None),
            P("section", "fsdp", None),
            P("section", "fsdp"),
        ),
        out_specs=(P("section", "fsdp", None), P("section", None)),
        check_vma=False,
    )
```

time: 386 us -> 298 us (0.77)
  matrix products: 77.2 us -> 29.3 us
  other arithmetic: 42.5 us -> 17.2 us
  waiting for transfers between devices: 163 us -> 177 us
  starting transfers between devices: 19.7 us -> 8.17 us
  blocking collectives: 40.1 us -> 33.3 us
  local copies, waits for them, and re-layouts: 23.4 us -> 17 us
    ppermute x10 -> x3, waiting for transfers between devices: 101 us -> 11 us  [on_device(): lax.ppermute(sent.astype(BF16), 'section', [(s, s - 1) for s in range(1,...]
    all_gather x1 -> x2, waiting for transfers between devices: 29.5 us -> 79 us  [the longest x1 43.9 us: on_device(): lax.all_gather(jnp.concatenate([w_scaled, w_back_own], axis=1), 'fsdp', a...]
    dot_general x67 -> x28, matrix products: 77.2 us -> 29.3 us  [the longest x12 21.4 us: dot(): return jnp.dot(left, right, preferred_element_type=F32)]
    reduce_scatter x1, waiting for transfers between devices: 31.6 us -> 77.6 us  [on_device(): total = lax.psum_scatter(term, 'fsdp', scatter_dimension=0, tiled=True)]
    psum x1 -> x0, blocking collectives: 27 us -> none  [on_device(): gain_sum = lax.psum(gain_acc, 'fsdp')]
    all_gather x1 -> x3, blocking collectives: 13.2 us -> 33.3 us  [the longest x1 12.7 us: on_device(): gain_sum = lax.all_gather(gain_rows, 'fsdp', axis=0, tiled=True)]
    convert_element_type x18 -> x12, other arithmetic: 17.5 us -> 2.88 us  [the longest x3 1.81 us: backward(): grad_att = grad_att.astype(BF16)]
    dynamic_update_slice x8 -> x0, other arithmetic: 14.5 us -> none  [work(): grad_store = lax.dynamic_update_index_in_dim(grad_store, grad_in, micro, 0)]
  transfers between devices with their start and end apart: 12 -> 7, of which waited for: 12 -> 6; matrix products, arithmetic and copies ran while one was open for 2% -> 5% of each run, Pallas kernels for 0% -> 0%
where the time goes in v1:
time: 298 us; the launch traced here: 296 us
  waiting for transfers between devices  177 us (59%)
  blocking collectives  33.3 us (11%)
  matrix products  29.3 us (10%)
  other arithmetic  17.2 us (6%)
  local copies, waits for them, and re-layouts  17 us (6%)
  between operations  14.4 us (5%)
  starting transfers between devices  8.17 us (3%)
    reduce_scatter x1, waiting for transfers between devices, on_device(): total = lax.psum_scatter(term, 'fsdp', scatter_dimension=0, tiled=True)  77.6 us
    all_gather x1, waiting for transfers between devices, on_device(): lax.all_gather(jnp.concatenate([w_scaled, w_back_own], axis=1), 'fsdp', a...  43.9 us
    all_gather x1, waiting for transfers between devices, on_device(): back_all = lax.all_gather(backs, 'fsdp', axis=0, tiled=True)  35 us
    dot_general x12, matrix products, dot(): return jnp.dot(left, right, preferred_element_type=F32)  21.4 us
    all_gather x1, blocking collectives, on_device(): gain_sum = lax.all_gather(gain_rows, 'fsdp', axis=0, tiled=True)  12.7 us
    ppermute x3, waiting for transfers between devices, on_device(): lax.ppermute(sent.astype(BF16), 'section', [(s, s - 1) for s in range(1,...  11 us
    all_gather x1, blocking collectives, on_device(): att_all = lax.all_gather(attended, 'section', axis=0)[:lower]  10.6 us
    all_gather x1, blocking collectives, on_device(): backs = lax.all_gather(w_back_own, 'section', axis=0)[:lower]  10.1 us
  transfers between devices with their start and end apart: 7, of which 6 were waited for; matrix products, arithmetic and copies ran while one was open for 5% of the time, Pallas kernels for 0%

profile of v1, /device:TPU:2, one launch (start us, length us, event | category | flops | bytes accessed | tf_op | source)
XLA Modules:
  0.0 296.3 jit_solution(16896579757957167068)
XLA Ops:
  7.2 1.4 copy.35
  8.7 10.1 %all-gather = bf16[2048,128]{0,1:T(8,128)(2,1)S(1)} all-gather(bf16[512,128]{0,1:T(8,128)(2,1)S(1)} %slice.150), channel_id=2, replica_groups=mesh['section'=4,'fsdp'=8] {'section'}, dimensions={0}, use_global_device_ids=true | all-gather | bytes 655360 | tf_op jit(solution)/shard_map/all_gather | solution.py:53
  18.7 0.2 copy.43
  19.0 0.9 copy.44
  20.1 0.8 pad_maximum_fusion.1
  21.0 2.1 multiply_reduce_fusion
  23.6 35.0 %all-gather.8.cloned.1.call-done = bf16[4096,384]{0,1:T(8,128)(2,1)} async-done(((bf16[512,384]{0,1:T(8,128)(2,1)}), bf16[4096,384]{0,1:T(8,128)(2,1)}) %all-gather.8.cloned.1.call-update) | async-done | bytes 3145744 | tf_op jit(solution)/shard_map/all_gather | solution.py:55
  58.7 4.3 %convolution_multiply_fusion = f32[256,384]{0,1:T(8,128)} fusion(bf16[256,4096]{1,0:T(8,128)(2,1)} %bitcast.79, bf16[4096,384]{0,1:T(8,128)(2,1)} %all-gather.8.cloned.1.call-done, f32[256]{0:T(256)S(1)} %rsqrt.15), kind=kOutput, calls=%fused_computation.21 | convolution fusion | flops 805404672 | bytes 5637120 | tf_op jit(solution)/shard_map/dot_general | solution.py:25
  62.9 43.9 %all-gather.6.cloned.1.call-done = bf16[4096,512]{0,1:T(8,128)(2,1)} async-done(((bf16[512,512]{0,1:T(8,128)(2,1)}), bf16[4096,512]{0,1:T(8,128)(2,1)}) %all-gather.6.cloned.1.call-update) | async-done | bytes 4194320 | tf_op jit(solution)/shard_map/all_gather | solution.py:50
  106.9 3.7 %fusion.16 = f32[256,384]{0,1:T(8,128)S(1)} fusion(bf16[256,4096]{1,0:T(8,128)(2,1)} %bitcast.80, bf16[4096,512]{0,1:T(8,128)(2,1)} %all-gather.6.cloned.1.call-done, f32[256]{0:T(256)S(1)} %rsqrt.15), kind=kOutput, calls=%fused_computation.23 | convolution fusion | flops 805404672 | bytes 5637120 | tf_op jit(solution)/shard_map/dot_general | solution.py:25
  110.7 0.3 fusion.72
  111.0 0.2 fusion.31
  111.2 0.8 convolution_bitcast_fusion.1
  112.0 0.3 multiply_reduce_fusion.7
  112.3 0.2 multiply_convert_fusion.4
  112.5 0.2 fusion.78
  112.7 0.2 fusion.82
  112.9 0.2 convolution_convert_fusion.6
  113.2 0.7 copy-done.11
  113.9 1.8 fusion.7
  115.7 1.0 fusion.19
  116.7 2.5 collective-permute-start
  119.2 7.6 %collective-permute-done = bf16[256,384]{0,1:T(8,128)(2,1)} collective-permute-done((bf16[256,384]{0,1:T(8,128)(2,1)}, bf16[256,384]{0,1:T(8,128)(2,1)}, u32[]{:S(2)}, u32[]{:S(2)}) %collective-permute-start) | collective-permute-done | bytes 196640 | tf_op jit(solution)/shard_map/ppermute | solution.py:112
  126.9 0.9 add_convert_fusion.4
  127.7 0.3 multiply_reduce_fusion.6
  128.0 0.2 multiply_convert_fusion.3
  128.2 0.2 fusion.79
  128.4 0.2 fusion.83
  128.5 0.2 convolution_convert_fusion.5
  129.0 1.9 add_convert_fusion.1
  130.9 1.9 collective-permute-start.1
  132.8 0.2 convolution_convert_fusion.2
  133.0 10.6 %all-gather.1 = bf16[1024,128]{1,0:T(8,128)(2,1)S(1)} all-gather(bf16[256,128]{1,0:T(8,128)(2,1)S(1)} %convolution_convert_fusion.2), channel_id=3, replica_groups=mesh['section'=4,'fsdp'=8] {'section'}, dimensions={0}, use_global_device_ids=true | all-gather | bytes 327680 | tf_op jit(solution)/shard_map/all_gather | solution.py:80
  143.6 0.7 slice.177
  144.3 1.7 copy.55
  146.0 0.9 add_convert_fusion.3
  147.0 0.3 multiply_reduce_fusion.5
  147.2 0.2 multiply_convert_fusion.2
  147.4 0.2 fusion.80
  147.8 0.2 convolution_convert_fusion.4
  148.2 1.2 add_convert_fusion
  149.5 3.6 %collective-permute-start.2 = (bf16[256,384]{0,1:T(8,128)(2,1)S(1)}, bf16[256,384]{0,1:T(8,128)(2,1)S(1)}, u32[]{:S(2)}, u32[]{:S(2)}) collective-permute-start(bf16[256,384]{0,1:T(8,128)(2,1)S(1)} %add_convert_fusion), channel_id=1, source_target_pairs={{8,0},{16,8},{24,16},{9,1},{17,9},{25,17},{10,2},{18,10},{26,18},{... | collective-permute-start | bytes 589832 | tf_op jit(solution)/shard_map/ppermute | solution.py:112
  153.1 1.4 fusion.1
  154.6 3.4 %collective-permute-done.2 = bf16[256,384]{0,1:T(8,128)(2,1)S(1)} collective-permute-done((bf16[256,384]{0,1:T(8,128)(2,1)S(1)}, bf16[256,384]{0,1:T(8,128)(2,1)S(1)}, u32[]{:S(2)}, u32[]{:S(2)}) %collective-permute-start.2) | collective-permute-done | bytes 196640 | tf_op jit(solution)/shard_map/ppermute | solution.py:112
  158.0 0.3 multiply_reduce_fusion.4
  158.2 0.2 multiply_convert_fusion.1
  158.4 0.2 fusion.81
  158.8 0.2 convolution_convert_fusion.3
  159.4 0.5 copy-done.7
  159.9 1.8 convolution_bitcast_fusion
  161.7 4.5 %copy-done.1 = f32[4096,768]{0,1:T(8,128)} copy-done((f32[4096,768]{0,1:T(8,128)}, f32[4096,768]{0,1:T(8,128)S(1)}, u32[]{:S(2)}) %copy-start.1) | copy-done | bytes 12582936
  166.2 2.1 slice.223
  168.3 7.6 %fusion = bf16[4096,384]{0,1:T(8,128)(2,1)} fusion(f32[4096,768]{0,1:T(8,128)} %copy-done.1, bf16[4096,512]{0,1:T(8,128)(2,1)} %all-gather.6.cloned.1.call-done, bf16[256,384]{0,1:T(8,128)(2,1)S(1)} %copy-done.8, bf16[256,384]{0,1:T(8,128)(2,1)S(1)} %get-tuple-element.9), kind=kOutput, calls=%fused_computation.3 | convolution fusion | flops 1286750208 | bytes 12976128 | tf_op jit(solution)/shard_map/dot_general | solution.py:25
  175.9 6.3 %pad_maximum_fusion = bf16[4096,896]{0,1:T(8,128)(2,1)} fusion(bf16[4096,384]{0,1:T(8,128)(2,1)} %fusion, bf16[4096,128]{0,1:T(8,128)(2,1)S(1)} %copy-done.3, bf16[4096,384]{0,1:T(8,128)(2,1)} %slice.223), kind=kLoop, calls=%fused_computation.1 | loop fusion | flops 22020096 | bytes 14680064 | tf_op jit(solution)/shard_map/concatenate | solution.py:122
  182.2 77.6 %reduce-scatter.5.cloned.1.call-done = bf16[512,896]{0,1:T(8,128)(2,1)} async-done(((bf16[4096,896]{0,1:T(8,128)(2,1)}), bf16[512,896]{0,1:T(8,128)(2,1)}) %reduce-scatter.5.cloned.1.call-update) | async-done | bytes 917520 | tf_op jit(solution)/shard_map/reduce_scatter | solution.py:130
  259.9 1.0 slice.182
  260.9 0.8 pad_bitcast_fusion
  261.8 2.0 fusion.23
  263.8 12.7 %all-gather.2 = f32[8,1,512]{2,1,0:T(1,128)S(1)} all-gather(f32[1,1,512]{2,1,0:T(1,128)S(1)} %bitcast.94), channel_id=1, replica_groups=mesh['section'=4,'fsdp'=8] {'fsdp'}, dimensions={0}, use_global_device_ids=true | all-gather | bytes 18432 | tf_op jit(solution)/shard_map/all_gather | solution.py:142
  276.5 9.2 %reduce-scatter.7.cloned.1.call-done = bf16[1,512,128]{1,2,0:T(8,128)(2,1)} async-done(((bf16[4,512,128]{1,2,0:T(8,128)(2,1)}), bf16[1,512,128]{1,2,0:T(8,128)(2,1)}) %reduce-scatter.7.cloned.1.call-update) | async-done | bytes 131088
  285.7 1.0 convert_add_fusion
  286.7 1.2 maximum_bitcast_fusion
  287.9 1.3 copy.56
  289.2 0.6 copy.62
  (84 shorter events, 2.2 us)
Async XLA Ops:
  7.2 104.0 %copy-start = (bf16[8,32,4096]{2,1,0:T(8,128)(2,1)S(1)}, bf16[8,32,4096]{2,1,0:T(8,128)(2,1)}, u32[]{:S(2)}) copy-start(bf16[8,32,4096]{2,1,0:T(8,128)(2,1)} %param.5) | copy-start | bytes 6291460
  7.2 12.8 %copy-start.10 = (bf16[1,512]{1,0:T(2,128)(2,1)S(1)}, bf16[1,512]{1,0:T(2,128)(2,1)}, u32[]{:S(2)}) copy-start(bf16[1,512]{1,0:T(2,128)(2,1)} %param.7) | copy-start | bytes 3076
  7.2 51.5 %all-gather.8.cloned.1.call-start = ((), (), s32[]{:S(2)}) async-start(), calls=%async_computation.3 | async-start | bytes 3538944 | tf_op jit(solution)/shard_map/all_gather | solution.py:55
  8.6 14.4 %copy-start.5 = (bf16[1,512,512]{1,2,0:T(8,128)(2,1)}, bf16[1,512,512]{1,2,0:T(8,128)(2,1)S(1)}, u32[]{:S(2)}) copy-start(bf16[1,512,512]{1,2,0:T(8,128)(2,1)S(1)} %copy.35) | copy-start | bytes 1572868
  19.9 86.9 %all-gather.6.cloned.1.call-start = ((), (), s32[]{:S(2)}) async-start(), calls=%async_computation.2 | async-start | bytes 4718592 | tf_op jit(solution)/shard_map/all_gather | solution.py:50
  20.9 238.9 %reduce-scatter.5.cloned.1.call-start = ((), (), s32[]{:S(2)}) async-start(), calls=%async_computation.4 | async-start | bytes 8257536 | tf_op jit(solution)/shard_map/reduce_scatter | solution.py:130
  106.9 4.3 %copy-start.4 = (bf16[4096,512]{0,1:T(8,128)(2,1)S(1)}, bf16[4096,512]{0,1:T(8,128)(2,1)}, u32[]{:S(2)}) copy-start(bf16[4096,512]{0,1:T(8,128)(2,1)} %all-gather.6.cloned.1.call-done) | copy-start | bytes 12582916
  112.0 1.9 copy-start.11
  113.9 1.8 copy-start.12
  115.7 1.0 copy-start.15
  116.7 10.1 %collective-permute-start = (bf16[256,384]{0,1:T(8,128)(2,1)}, bf16[256,384]{0,1:T(8,128)(2,1)}, u32[]{:S(2)}, u32[]{:S(2)}) collective-permute-start(bf16[256,384]{0,1:T(8,128)(2,1)} %fusion.19), channel_id=1, source_target_pairs={{8,0},{16,8},{24,16},{9,1},{17,9},{25,17},{10,2},{18,10},{26,18},{... | collective-permute-start | bytes 589832 | tf_op jit(solution)/shard_map/ppermute | solution.py:112
  119.2 9.8 %copy-start.13 = (f32[256,384]{0,1:T(8,128)S(1)}, f32[256,384]{0,1:T(8,128)}, u32[]{:S(2)}) copy-start(f32[256,384]{0,1:T(8,128)} %convolution_multiply_fusion) | copy-start | bytes 1179652
  119.2 9.8 %copy-start.16 = (bf16[384,384]{1,0:T(8,128)(2,1)S(1)}, bf16[384,384]{1,0:T(8,128)(2,1)}, u32[]{:S(2)}) copy-start(bf16[384,384]{1,0:T(8,128)(2,1)} %copy-done.15) | copy-start | bytes 884740
  130.9 15.2 %collective-permute-start.1 = (bf16[256,384]{0,1:T(8,128)(2,1)}, bf16[256,384]{0,1:T(8,128)(2,1)}, u32[]{:S(2)}, u32[]{:S(2)}) collective-permute-start(bf16[256,384]{0,1:T(8,128)(2,1)} %add_convert_fusion.1), channel_id=1, source_target_pairs={{8,0},{16,8},{24,16},{9,1},{17,9},{25,17},{10,2},{18,10},{26,18},{... | collective-permute-start | bytes 589832 | tf_op jit(solution)/shard_map/ppermute | solution.py:112
  146.0 2.2 copy-start.14
  146.0 2.2 copy-start.17
  149.5 8.5 %collective-permute-start.2 = (bf16[256,384]{0,1:T(8,128)(2,1)S(1)}, bf16[256,384]{0,1:T(8,128)(2,1)S(1)}, u32[]{:S(2)}, u32[]{:S(2)}) collective-permute-start(bf16[256,384]{0,1:T(8,128)(2,1)S(1)} %add_convert_fusion), channel_id=1, source_target_pairs={{8,0},{16,8},{24,16},{9,1},{17,9},{25,17},{10,2},{18,10},{26,18},{... | collective-permute-start | bytes 589832 | tf_op jit(solution)/shard_map/ppermute | solution.py:112
  154.6 4.7 %copy-start.9 = (bf16[3,256,128]{1,2,0:T(8,128)(2,1)S(1)}, bf16[3,256,128]{1,2,0:T(8,128)(2,1)}, u32[]{:S(2)}) copy-start(bf16[3,256,128]{1,2,0:T(8,128)(2,1)} %copy.55) | copy-start | bytes 589828
  158.0 1.9 copy-start.2
  159.2 0.7 copy-start.7
  161.7 4.5 %copy-start.1 = (f32[4096,768]{0,1:T(8,128)}, f32[4096,768]{0,1:T(8,128)S(1)}, u32[]{:S(2)}) copy-start(f32[4096,768]{0,1:T(8,128)S(1)} %convolution_bitcast_fusion) | copy-start | bytes 37748740
  166.2 2.1 copy-start.8
  168.3 7.6 %copy-start.3 = (bf16[4096,128]{0,1:T(8,128)(2,1)S(1)}, bf16[4096,128]{0,1:T(8,128)(2,1)}, u32[]{:S(2)}) copy-start(bf16[4096,128]{0,1:T(8,128)(2,1)} %fusion.1) | copy-start | bytes 3145732
  182.2 79.6 %copy-start.6 = (bf16[1,512,512]{1,2,0:T(8,128)(2,1)S(1)}, bf16[1,512,512]{1,2,0:T(8,128)(2,1)}, u32[]{:S(2)}) copy-start(bf16[1,512,512]{1,2,0:T(8,128)(2,1)} %copy-done.5) | copy-start | bytes 1572868
  182.2 103.5 %reduce-scatter.7.cloned.1.call-start = ((), (), s32[]{:S(2)}) async-start(), calls=%async_computation.5 | async-start | bytes 655360
Sparse Core Ops, SparseCore 0:
  20.1 38.5 all-gather.7
  60.8 46.0 all-gather.5
  182.3 77.5 reduce-scatter.4
  262.5 23.0 reduce-scatter.6

commit v2 on v1

--- a/solution.py
+++ b/solution.py
@@ -1,7 +1,14 @@
+import functools
+
 import jax
 import jax.numpy as jnp
 from jax import lax
+from jax.experimental import pallas as pl
+from jax.experimental.pallas import tpu as pltpu
 from jax.sharding import PartitionSpec as P
+
+MESH = pl.DeviceIdType.MESH
+VMEM_BYTES = 56 * 1024 * 1024
 
 F32 = jnp.float32
 BF16 = jnp.bfloat16
@@ -31,6 +38,228 @@
 
 def dot_cols(left, right):
     return lax.dot_general(left, right, (((1,), (1,)), ((), ())), preferred_element_type=F32)
+
+
+def remote(src, dst, send_sem, recv_sem, section, member):
+    return pltpu.make_async_remote_copy(
+        src_ref=src,
+        dst_ref=dst,
+        send_sem=send_sem,
+        recv_sem=recv_sem,
+        device_id=(section, member),
+        device_id_type=MESH,
+    )
+
+
+def greet(sections, chips, here, chip, core):
+    barrier = pltpu.get_barrier_semaphore()
+
+    def hello(section, member):
+        pl.semaphore_signal(barrier, inc=1, device_id=(section, member), device_id_type=MESH)
+
+    @pl.when(chip > 0)
+    def _():
+        hello(here, (chip - 1) * 2 + core)
+
+    @pl.when(chip < chips - 1)
+    def _():
+        hello(here, (chip + 1) * 2 + core)
+
+    hello(here, chip * 2 + 1 - core)
+
+    @pl.loop(1, sections)
+    def _(step):
+        hello(lax.rem(here + step, sections), chip * 2 + core)
+
+    pl.semaphore_wait(
+        barrier,
+        sections + (chip > 0).astype(jnp.int32) + (chip < chips - 1).astype(jnp.int32),
+    )
+
+
+def gather_kernel(
+    sections,
+    chips,
+    w_ref,
+    x_ref,
+    up_ref,
+    full,
+    proj,
+    through,
+    cross,
+    back,
+    z_recv,
+    z_right,
+    z_left,
+    sib_recv,
+    sib_send,
+    x_recv,
+    x_send,
+    sibx_recv,
+    sibx_send,
+):
+    here = lax.axis_index("section")
+    member = lax.axis_index("fsdp")
+    chip = member // 2
+    core = member % 2
+    sibling = chip * 2 + 1 - core
+    rows = w_ref.shape[0]
+    head = w_ref.shape[1] // 4
+    full[member] = w_ref[...]
+    proj[...] = jnp.zeros_like(proj)
+    through[...] = jnp.zeros_like(through)
+    cross[...] = jnp.zeros_like(cross)
+    greet(sections, chips, here, chip, core)
+
+    def to_right(b):
+        block = full.at[b * 2 + core]
+        return remote(block, block, z_right.at[b], z_recv.at[b], here, member + 2)
+
+    def to_left(b):
+        block = full.at[b * 2 + core]
+        return remote(block, block, z_left.at[b], z_recv.at[b], here, member - 2)
+
+    def to_sibling(b, lane):
+        block = full.at[b * 2 + lane]
+        return remote(block, block, sib_send.at[b], sib_recv.at[b], here, sibling)
+
+    def to_section(b, source, section):
+        return remote(
+            full.at[b * 2 + core, :, pl.ds(3 * head, head)],
+            back.at[source, b * 2 + core],
+            x_send.at[section, b],
+            x_recv.at[source, b],
+            section,
+            member,
+        )
+
+    def back_to_sibling(b, source, lane):
+        block = back.at[source, b * 2 + lane]
+        return remote(
+            block, block, sibx_send.at[source, b], sibx_recv.at[source, b], here, sibling
+        )
+
+    def columns(idx):
+        return pl.ds(pl.multiple_of(idx * rows, rows), rows)
+
+    def products(idx):
+        proj[:, : 3 * head] += dot(x_ref[:, columns(idx)], full[idx, :, : 3 * head])
+        proj[:, 3 * head :] += dot(up_ref[:, columns(idx)], full[idx, :, 3 * head :])
+
+    def back_products(source, idx):
+        through[source] += dot(x_ref[:, columns(idx)], back[source, idx])
+        cross[source] += dot_rows(full[idx, :, : 3 * head], back[source, idx])
+
+    def arrived(b):
+        @pl.when(b < chip)
+        def _():
+            to_right(b).wait_recv()
+
+        @pl.when(b > chip)
+        def _():
+            to_left(b).wait_recv()
+
+        @pl.when(jnp.logical_and(b <= chip, chip < chips - 1))
+        def _():
+            to_right(b).start()
+
+        @pl.when(jnp.logical_and(b >= chip, chip > 0))
+        def _():
+            to_left(b).start()
+
+        to_sibling(b, core).start()
+
+        @pl.loop(here + 1, sections)
+        def _(section):
+            to_section(b, here, section).start()
+
+        products(b * 2 + core)
+
+    def second(b):
+        to_sibling(b, 1 - core).wait_recv()
+        products(b * 2 + 1 - core)
+
+        @pl.loop(0, here)
+        def _(source):
+            to_section(b, source, here).wait_recv()
+            back_to_sibling(b, source, core).start()
+            back_products(source, b * 2 + core)
+
+    def third(b):
+        @pl.loop(0, here)
+        def _(source):
+            back_to_sibling(b, source, 1 - core).wait_recv()
+            back_products(source, b * 2 + 1 - core)
+
+    def done(b):
+        @pl.when(jnp.logical_and(b <= chip, chip < chips - 1))
+        def _():
+            to_right(b).wait_send()
+
+        @pl.when(jnp.logical_and(b >= chip, chip > 0))
+        def _():
+            to_left(b).wait_send()
+
+        to_sibling(b, core).wait_send()
+
+        @pl.loop(here + 1, sections)
+        def _(section):
+            to_section(b, here, section).wait_send()
+
+        @pl.loop(0, here)
+        def _(source):
+            back_to_sibling(b, source, core).wait_send()
+
+    @pl.loop(0, 2 * (chips + 2))
+    def _(turn_no):
+        side = turn_no % 2
+        for lag, act in enumerate((arrived, second, third)):
+            away = turn_no // 2 - lag
+            b = jnp.where(side == 1, chip + away, chip - away)
+            first = jnp.where(side == 1, 1, 0)
+            fits = jnp.logical_and(b >= 0, b < chips)
+            pl.when(jnp.logical_and(fits, away >= first))(functools.partial(act, b))
+
+    pl.loop(0, chips)(done)
+
+
+def gathered(sections, members, w_rows, x, up):
+    rows, cols = w_rows.shape
+    head = cols // 4
+    tokens = x.shape[0]
+    chips = members // 2
+    lower = sections - 1
+    vmem = pl.BlockSpec(memory_space=pltpu.VMEM)
+    dma = pltpu.SemaphoreType.DMA
+    return pl.pallas_call(
+        functools.partial(gather_kernel, sections, chips),
+        out_shape=(
+            jax.ShapeDtypeStruct((members, rows, cols), BF16),
+            jax.ShapeDtypeStruct((tokens, cols), F32),
+            jax.ShapeDtypeStruct((lower, tokens, head), F32),
+            jax.ShapeDtypeStruct((lower, 3 * head, head), F32),
+        ),
+        in_specs=[vmem] * 3,
+        out_specs=(vmem,) * 4,
+        scratch_shapes=[
+            pltpu.VMEM((lower, members, rows, head), BF16),
+            dma((chips,)),
+            dma((chips,)),
+            dma((chips,)),
+            dma((chips,)),
+            dma((chips,)),
+            dma((lower, chips)),
+            dma((sections, chips)),
+            dma((lower, chips)),
+            dma((lower, chips)),
+        ],
+        compiler_params=pltpu.CompilerParams(
+            collective_id=0, has_side_effects=True, vmem_limit_bytes=VMEM_BYTES
+        ),
+        cost_estimate=pl.CostEstimate(
+            flops=2 * tokens * members * rows * cols, bytes_accessed=1 << 23, transcendentals=0
+        ),
+    )(w_rows, x, up)
 
 
 def on_device(inputs, upstream, weights, gain):
@@ -47,19 +276,15 @@
     w_scaled = (w_own[:, : 3 * head] * gain_own).astype(BF16)
     w_back_own = weights[0][:, 3 * head :]
 
-    w_full = lax.all_gather(
-        jnp.concatenate([w_scaled, w_back_own], axis=1), "fsdp", axis=0, tiled=True
-    )
-    backs = lax.all_gather(w_back_own, "section", axis=0)[:lower]
-    backs = jnp.transpose(backs, (1, 0, 2)).reshape(w_back_own.shape[0], lower * head)
-    back_all = lax.all_gather(backs, "fsdp", axis=0, tiled=True)
-    wg = w_full[:, : 3 * head]
-    wb = w_full[:, 3 * head :]
-
+    members = lax.axis_size("fsdp")
+    full, products, through, cross = gathered(
+        sections, members, jnp.concatenate([w_scaled, w_back_own], axis=1), x, up
+    )
+    wg = full.reshape(width, 4 * head)[:, : 3 * head]
     xfloat = x.astype(F32)
     inv = lax.rsqrt(jnp.mean(xfloat * xfloat, axis=1, keepdims=True) + 1e-05)
-    proj = dot(x, wg) * inv
-    direct = dot(up, wb)
+    proj = products[:, : 3 * head] * inv
+    direct = products[:, 3 * head :]
 
     cosine, sine = rope_tables(length, head)
     cos_full = jnp.tile(jnp.concatenate([cosine, cosine], axis=1), (micro_count, 1))
@@ -80,8 +305,8 @@
     att_all = lax.all_gather(attended, "section", axis=0)[:lower]
     att_all = jnp.transpose(att_all, (1, 0, 2)).reshape(tokens, lower * head)
 
-    cross = dot_rows(wg, back_all).astype(BF16)
-    through = dot(x, back_all) * inv
+    cross = jnp.transpose(cross, (1, 0, 2)).reshape(3 * head, lower * head).astype(BF16)
+    through = jnp.transpose(through, (1, 0, 2)).reshape(tokens, lower * head) * inv
 
     def backward(grad_att):
         grad_att = grad_att.astype(BF16)

time: 298 us -> 254 us (0.85)
  waiting for transfers between devices: 177 us -> 105 us
  Pallas kernels: 0 us -> 50.6 us
  matrix products: 29.3 us -> 18.4 us
  blocking collectives: 33.3 us -> 22.9 us
    all_gather x2 -> x0, waiting for transfers between devices: 79 us -> none  [the longest x1 43.9 us: on_device(): lax.all_gather(jnp.concatenate([w_scaled, w_back_own], axis=1), 'fsdp', a...]
    pallas_call x0 -> x1, Pallas kernels: none -> 50.6 us  [gathered(): pl.pallas_call(functools.partial(gather_kernel, sections, chips), out_sha...]
    dot_general x12 -> x9, matrix products: 21.4 us -> 10.4 us  [dot(): return jnp.dot(left, right, preferred_element_type=F32)]
    all_gather x1 -> x0, blocking collectives: 10.1 us -> none  [on_device(): backs = lax.all_gather(w_back_own, 'section', axis=0)[:lower]]
    ppermute x3, waiting for transfers between devices: 11 us -> 15.6 us  [on_device(): lax.ppermute(sent.astype(BF16), 'section', [(s, s - 1) for s in range(1,...]
    unnamed x39 -> x53, local copies, waits for them, and re-layouts: 9.07 us -> 6.42 us
    unnamed x5 -> x3, waiting for transfers between devices: 9.28 us -> 11.1 us
    dot_general x11 -> x10, matrix products: 6.58 us -> 5.15 us  [dot_rows(): lax.dot_general(left, right, (((0,), (0,)), ((), ())), preferred_element_...]
  transfers between devices with their start and end apart: 7 -> 5, of which waited for: 6 -> 4; matrix products, arithmetic and copies ran while one was open for 5% -> 3% of each run, Pallas kernels for 0% -> 0%
where the time goes in v2:
time: 254 us; the launch traced here: 252 us
  waiting for transfers between devices  105 us (41%)
  Pallas kernels  50.6 us (20%)
  blocking collectives  22.9 us (9%)
  other arithmetic  18.5 us (7%)
  matrix products  18.4 us (7%)
  local copies, waits for them, and re-layouts  15.7 us (6%)
  between operations  14.8 us (6%)
  starting transfers between devices  5.96 us (2%)
    reduce_scatter x1, waiting for transfers between devices, on_device(): total = lax.psum_scatter(term, 'fsdp', scatter_dimension=0, tiled=True)  78.2 us
    pallas_call x1, Pallas kernels, gathered(): pl.pallas_call(functools.partial(gather_kernel, sections, chips), out_sha...  50.6 us
    ppermute x3, waiting for transfers between devices, on_device(): lax.ppermute(sent.astype(BF16), 'section', [(s, s - 1) for s in range(1,...  15.6 us
    all_gather x1, blocking collectives, on_device(): gain_sum = lax.all_gather(gain_rows, 'fsdp', axis=0, tiled=True)  12.7 us
    unnamed x3, waiting for transfers between devices  11.1 us
    dot_general x9, matrix products, dot(): return jnp.dot(left, right, preferred_element_type=F32)  10.4 us
    all_gather x1, blocking collectives, on_device(): att_all = lax.all_gather(attended, 'section', axis=0)[:lower]  10.2 us
    unnamed x53, local copies, waits for them, and re-layouts  6.42 us
  transfers between devices with their start and end apart: 5, of which 4 were waited for; matrix products, arithmetic and copies ran while one was open for 3% of the time, Pallas kernels for 0%

profile of v2, /device:TPU:2, one launch (start us, length us, event | category | flops | bytes accessed | tf_op | source)
XLA Modules:
  0.0 251.5 jit_solution(18139614709980173968)
XLA Ops:
  7.3 0.7 convert_element_type.172
  8.0 0.9 slice.149
  8.9 1.1 fusion.8
  10.0 2.1 multiply_reduce_fusion
  12.2 0.8 pad_maximum_fusion.1.w_ref
  13.0 50.6 %shard_map.59 = (bf16[8,512,512]{2,1,0:T(8,128)(2,1)}, f32[256,512]{1,0:T(8,128)}, f32[3,256,128]{2,1,0:T(8,128)}, f32[3,384,128]{2,1,0:T(8,128)}) custom-call(bf16[512,512]{1,0:T(8,128)(2,1)} %pad_maximum_fusion.1.w_ref, bf16[256,4096]{1,0:T(8,128)(2,1)} %bitcast.156, bf16[256,4096]{1,0:T(8,128)(2,1)} %bitcast.158), custom_call_target="tpu_custom_call" | custom-call | flops 1073741824 | bytes 8388608 | tf_op jit(solution)/shard_map/pallas_call | solution.py:234
  63.6 1.2 slice_multiply_fusion
  65.3 0.2 fusion.68
  65.5 0.2 fusion.25
  65.7 1.1 multiply_reduce_fusion.7
  66.8 0.2 multiply_convert_fusion.4
  67.0 0.2 fusion.75
  67.2 0.2 fusion.74
  67.6 0.2 convolution_convert_fusion.6
  68.0 0.2 multiply_reduce_fusion.3
  68.6 0.2 copy.83
  68.8 0.3 fusion.6
  69.1 1.9 collective-permute-start
  71.1 8.8 %collective-permute-done = bf16[256,384]{1,0:T(8,128)(2,1)S(1)} collective-permute-done((bf16[256,384]{1,0:T(8,128)(2,1)S(1)}, bf16[256,384]{1,0:T(8,128)(2,1)S(1)}, u32[]{:S(2)}, u32[]{:S(2)}) %collective-permute-start) | collective-permute-done | bytes 196640 | tf_op jit(solution)/shard_map/ppermute | solution.py:337
  79.9 0.2 multiply_reduce_fusion.6
  80.1 0.2 multiply_convert_fusion.3
  80.3 0.2 fusion.77
  80.5 0.2 fusion.76
  81.2 0.2 multiply_reduce_fusion.2
  81.5 0.3 add_convert_fusion.1
  81.8 2.1 collective-permute-start.1
  83.8 0.2 convolution_convert_fusion.2
  84.1 6.8 %collective-permute-done.1 = bf16[256,384]{1,0:T(8,128)(2,1)S(1)} collective-permute-done((bf16[256,384]{1,0:T(8,128)(2,1)S(1)}, bf16[256,384]{1,0:T(8,128)(2,1)S(1)}, u32[]{:S(2)}, u32[]{:S(2)}) %collective-permute-start.1) | collective-permute-done | bytes 196640 | tf_op jit(solution)/shard_map/ppermute | solution.py:337
  90.9 0.2 multiply_reduce_fusion.5
  91.2 0.2 multiply_convert_fusion.2
  91.5 0.2 fusion.78
  91.7 0.2 convolution_convert_fusion.4
  92.3 0.2 multiply_reduce_fusion.1
  92.5 1.0 add_convert_fusion
  93.5 1.9 collective-permute-start.2
  95.4 1.9 fusion.1
  97.4 10.2 %all-gather = bf16[1024,128]{1,0:T(8,128)(2,1)S(1)} all-gather(bf16[256,128]{1,0:T(8,128)(2,1)} %copy-done.10), channel_id=2, replica_groups=mesh['section'=4,'fsdp'=8] {'section'}, dimensions={0}, use_global_device_ids=true | all-gather | bytes 327680 | tf_op jit(solution)/shard_map/all_gather | solution.py:305
  107.5 0.7 slice.173
  108.2 1.7 copy.107
  110.0 1.7 copy.108
  111.7 0.9 add_convert_fusion.2
  112.7 1.0 multiply_reduce_fusion.4
  113.7 0.9 multiply_convert_fusion.1
  114.6 0.2 fusion.81
  114.8 0.2 fusion.80
  115.0 0.2 convolution_convert_fusion.3
  115.6 0.2 fusion.10
  116.0 0.5 copy-done.4
  116.5 1.9 convolution_bitcast_fusion
  118.4 4.5 %copy-done = f32[4096,768]{1,0:T(8,128)} copy-done((f32[4096,768]{1,0:T(8,128)}, f32[4096,768]{1,0:T(8,128)S(1)}, u32[]{:S(2)}) %copy-start) | copy-done | bytes 12582936
  122.9 0.3 slice.207
  123.2 0.6 copy-done.5
  123.9 7.7 %fusion = bf16[4096,384]{1,0:T(8,128)(2,1)} fusion(f32[4096,768]{1,0:T(8,128)} %copy-done, bf16[4096,512]{1,0:T(8,128)(2,1)} %bitcast.160, bf16[256,384]{1,0:T(8,128)(2,1)S(1)} %copy-done.5, bf16[256,384]{1,0:T(8,128)(2,1)S(1)} %copy-done.7, pred[384]{0:T(512)(128)(4,1)S(1)} %copy-done.25), kind=kOutput, calls=%fused_computation.3 | convolution fusion | flops 1286848512 | bytes 12976512 | tf_op jit(solution)/shard_map/dot_general | solution.py:32
  131.6 5.7 %pad_maximum_fusion = bf16[4096,896]{1,0:T(8,128)(2,1)} fusion(bf16[4096,384]{1,0:T(8,128)(2,1)} %fusion, bf16[4096,128]{1,0:T(8,128)(2,1)} %fusion.1, bf16[4096,384]{1,0:T(8,128)(2,1)S(1)} %slice.207), kind=kLoop, calls=%fused_computation.1 | loop fusion | flops 22020096 | bytes 14680064 | tf_op jit(solution)/shard_map/concatenate | solution.py:347
  137.4 78.2 %reduce-scatter.5.cloned.1.call-done = bf16[512,896]{1,0:T(8,128)(2,1)} async-done(((bf16[4096,896]{1,0:T(8,128)(2,1)}), bf16[512,896]{1,0:T(8,128)(2,1)}) %reduce-scatter.5.cloned.1.call-update) | async-done | bytes 917520 | tf_op jit(solution)/shard_map/reduce_scatter | solution.py:355
  215.6 1.1 slice.179
  216.7 0.2 copy.112
  216.9 1.0 copy.113
  218.0 0.3 fusion.9
  218.3 12.7 %all-gather.1 = f32[8,1,512]{2,1,0:T(1,128)S(1)} all-gather(f32[1,1,512]{2,1,0:T(1,128)S(1)} %bitcast.175), channel_id=1, replica_groups=mesh['section'=4,'fsdp'=8] {'fsdp'}, dimensions={0}, use_global_device_ids=true | all-gather | bytes 18432 | tf_op jit(solution)/shard_map/all_gather | solution.py:367
  231.0 11.1 %reduce-scatter.7.cloned.1.call-done = bf16[1,512,128]{2,1,0:T(8,128)(2,1)} async-done(((bf16[4,512,128]{2,1,0:T(8,128)(2,1)}), bf16[1,512,128]{2,1,0:T(8,128)(2,1)}) %reduce-scatter.7.cloned.1.call-update) | async-done | bytes 131088
  242.1 0.9 convert_add_fusion
  243.0 1.1 maximum_bitcast_fusion
  244.1 0.6 copy.130
  (89 shorter events, 3.1 us)
Async XLA Ops:
  7.2 208.4 %reduce-scatter.5.cloned.1.call-start = ((), (), s32[]{:S(2)}) async-start(), calls=%async_computation.2 | async-start | bytes 8257536 | tf_op jit(solution)/shard_map/reduce_scatter | solution.py:355
  7.2 83.9 %copy-start.15 = (s32[256]{0:T(256)}, s32[256]{0:T(256)S(1)}, u32[]{:S(2)}) copy-start(s32[256]{0:T(256)S(1)} %get-tuple-element.61) | copy-start | bytes 3076
  7.2 83.9 %copy-start.16 = (s32[256]{0:T(256)}, s32[256]{0:T(256)S(1)}, u32[]{:S(2)}) copy-start(s32[256]{0:T(256)S(1)} %get-tuple-element.62) | copy-start | bytes 3076
  7.3 83.9 %copy-start.17 = (pred[256]{0:T(512)(128)(4,1)}, pred[256]{0:T(512)(128)(4,1)S(1)}, u32[]{:S(2)}) copy-start(pred[256]{0:T(512)(128)(4,1)S(1)} %compare_and_fusion) | copy-start | bytes 772
  8.0 55.6 %copy-start.22 = (f32[1,512]{1,0:T(1,128)}, f32[1,512]{1,0:T(1,128)S(1)}, u32[]{:S(2)}) copy-start(f32[1,512]{1,0:T(1,128)S(1)} %convert_element_type.172) | copy-start | bytes 6148
  12.2 80.3 %copy-start.18 = (f32[256]{0:T(256)}, f32[256]{0:T(256)S(1)}, u32[]{:S(2)}) copy-start(f32[256]{0:T(256)S(1)} %rsqrt.15) | copy-start | bytes 3076
  63.6 4.0 %copy-start.2 = (f32[256,512]{1,0:T(8,128)S(1)}, f32[256,512]{1,0:T(8,128)}, u32[]{:S(2)}) copy-start(f32[256,512]{1,0:T(8,128)} %get-tuple-element.6) | copy-start | bytes 1572868
  64.9 3.3 %copy-start.14 = (f32[3,256,128]{2,1,0:T(8,128)S(1)}, f32[3,256,128]{2,1,0:T(8,128)}, u32[]{:S(2)}) copy-start(f32[3,256,128]{2,1,0:T(8,128)} %get-tuple-element.8) | copy-start | bytes 1179652
  65.1 27.0 %copy-start.12 = (f32[32,128]{1,0:T(8,128)}, f32[32,128]{1,0:T(8,128)S(1)}, u32[]{:S(2)}) copy-start(f32[32,128]{1,0:T(8,128)S(1)} %get-tuple-element.60) | copy-start | bytes 49156
  65.5 25.7 %copy-start.20 = (f32[256]{0:T(256)}, f32[256]{0:T(256)S(1)}, u32[]{:S(2)}) copy-start(f32[256]{0:T(256)S(1)} %get-tuple-element.49) | copy-start | bytes 3076
  65.5 3.0 %copy-start.11 = (f32[3,384,128]{2,1,0:T(8,128)S(1)}, f32[3,384,128]{2,1,0:T(8,128)}, u32[]{:S(2)}) copy-start(f32[3,384,128]{2,1,0:T(8,128)} %get-tuple-element.7) | copy-start | bytes 1769476
  65.7 25.5 %copy-start.21 = (f32[256]{0:T(256)}, f32[256]{0:T(256)S(1)}, u32[]{:S(2)}) copy-start(f32[256]{0:T(256)S(1)} %fusion.25) | copy-start | bytes 3076
  69.1 10.7 %collective-permute-start = (bf16[256,384]{1,0:T(8,128)(2,1)S(1)}, bf16[256,384]{1,0:T(8,128)(2,1)S(1)}, u32[]{:S(2)}, u32[]{:S(2)}) collective-permute-start(bf16[256,384]{1,0:T(8,128)(2,1)S(1)} %fusion.6), channel_id=1, source_target_pairs={{8,0},{16,8},{24,16},{9,1},{17,9},{25,17},{10,2},{18,10},{26,18},{... | collective-permute-start | bytes 589832 | tf_op jit(solution)/shard_map/ppermute | solution.py:337
  81.8 13.7 %copy-start.3 = (bf16[8,32,4096]{2,1,0:T(8,128)(2,1)S(1)}, bf16[8,32,4096]{2,1,0:T(8,128)(2,1)}, u32[]{:S(2)}) copy-start(bf16[8,32,4096]{2,1,0:T(8,128)(2,1)} %param.5) | copy-start | bytes 6291460
  81.8 9.1 %collective-permute-start.1 = (bf16[256,384]{1,0:T(8,128)(2,1)S(1)}, bf16[256,384]{1,0:T(8,128)(2,1)S(1)}, u32[]{:S(2)}, u32[]{:S(2)}) collective-permute-start(bf16[256,384]{1,0:T(8,128)(2,1)S(1)} %add_convert_fusion.1), channel_id=1, source_target_pairs={{8,0},{16,8},{24,16},{9,1},{17,9},{25,17},{10,2},{18,10},{26,18},{... | collective-permute-start | bytes 589832 | tf_op jit(solution)/shard_map/ppermute | solution.py:337
  84.1 11.3 %copy-start.10 = (bf16[256,128]{1,0:T(8,128)(2,1)}, bf16[256,128]{1,0:T(8,128)(2,1)S(1)}, u32[]{:S(2)}) copy-start(bf16[256,128]{1,0:T(8,128)(2,1)S(1)} %convolution_convert_fusion.2) | copy-start | bytes 196612
  93.5 18.2 %collective-permute-start.2 = (bf16[256,384]{1,0:T(8,128)(2,1)}, bf16[256,384]{1,0:T(8,128)(2,1)}, u32[]{:S(2)}, u32[]{:S(2)}) collective-permute-start(bf16[256,384]{1,0:T(8,128)(2,1)} %add_convert_fusion), channel_id=1, source_target_pairs={{8,0},{16,8},{24,16},{9,1},{17,9},{25,17},{10,2},{18,10},{26,18},{... | collective-permute-start | bytes 589832 | tf_op jit(solution)/shard_map/ppermute | solution.py:337
  97.4 19.1 %copy-start.1 = (bf16[1,8,32,4096]{3,2,1,0:T(8,128)(2,1)S(1)}, bf16[1,8,32,4096]{3,2,1,0:T(8,128)(2,1)}, u32[]{:S(2)}) copy-start(bf16[1,8,32,4096]{3,2,1,0:T(8,128)(2,1)} %param.4) | copy-start | bytes 6291460
  111.7 3.7 %copy-start.13 = (f32[32,128]{1,0:T(8,128)S(1)}, f32[32,128]{1,0:T(8,128)}, u32[]{:S(2)}) copy-start(f32[32,128]{1,0:T(8,128)} %copy-done.12) | copy-start | bytes 49156
  111.7 3.9 %copy-start.19 = (f32[256]{0:T(256)S(1)}, f32[256]{0:T(256)}, u32[]{:S(2)}) copy-start(f32[256]{0:T(256)} %copy-done.18) | copy-start | bytes 3076
  111.7 4.1 %copy-start.6 = (bf16[256,384]{1,0:T(8,128)(2,1)S(1)}, bf16[256,384]{1,0:T(8,128)(2,1)}, u32[]{:S(2)}) copy-start(bf16[256,384]{1,0:T(8,128)(2,1)} %copy.108) | copy-start | bytes 589828
  111.7 4.2 %copy-start.24 = (pred[384]{0:T(512)(128)(4,1)}, pred[384]{0:T(512)(128)(4,1)S(1)}, u32[]{:S(2)}) copy-start(pred[384]{0:T(512)(128)(4,1)S(1)} %iota_compare_fusion.1) | copy-start | bytes 1156
  115.8 0.7 copy-start.4
  118.4 4.5 %copy-start = (f32[4096,768]{1,0:T(8,128)}, f32[4096,768]{1,0:T(8,128)S(1)}, u32[]{:S(2)}) copy-start(f32[4096,768]{1,0:T(8,128)S(1)} %convolution_bitcast_fusion) | copy-start | bytes 37748740
  122.9 0.9 copy-start.5
  122.9 1.0 copy-start.7
  122.9 1.0 copy-start.25
  137.3 80.7 %copy-start.8 = (bf16[1,512,512]{2,1,0:T(8,128)(2,1)S(1)}, bf16[1,512,512]{2,1,0:T(8,128)(2,1)}, u32[]{:S(2)}) copy-start(bf16[1,512,512]{2,1,0:T(8,128)(2,1)} %param.6) | copy-start | bytes 1572868
  137.3 80.7 %copy-start.23 = (f32[1,512]{1,0:T(1,128)S(1)}, f32[1,512]{1,0:T(1,128)}, u32[]{:S(2)}) copy-start(f32[1,512]{1,0:T(1,128)} %copy-done.22) | copy-start | bytes 6148
  137.3 104.8 %reduce-scatter.7.cloned.1.call-start = ((), (), s32[]{:S(2)}) async-start(), calls=%async_computation.3 | async-start | bytes 655360
  215.6 2.4 copy-start.9
Sparse Core Ops, SparseCore 0:
  137.4 78.0 reduce-scatter.4
  218.9 23.0 reduce-scatter.6

commit v3 on v2

--- a/solution.py
+++ b/solution.py
@@ -262,6 +262,280 @@
     )(w_rows, x, up)
 
 
+def scatter_kernel(
+    sections,
+    chips,
+    x_ref,
+    up_ref,
+    full,
+    own_rhs,
+    low_rhs,
+    mixed,
+    att,
+    w_ref,
+    gain_ref,
+    out,
+    gains,
+    acc,
+    sib_out,
+    sib_in,
+    sibx_out,
+    sibx_in,
+    x_in,
+    z_out,
+    z_in,
+    sib_send,
+    sib_recv,
+    sibx_send,
+    sibx_recv,
+    x_send,
+    x_recv,
+    z_send,
+    z_recv,
+    g_send,
+    g_recv,
+):
+    here = lax.axis_index("section")
+    member = lax.axis_index("fsdp")
+    members = 2 * chips
+    chip = member // 2
+    core = member % 2
+    sibling = chip * 2 + 1 - core
+    rows = w_ref.shape[0]
+    head = w_ref.shape[1] // 4
+    wide = pl.ds(0, 3 * head)
+    last = pl.ds(3 * head, head)
+
+    barrier = pltpu.get_barrier_semaphore()
+
+    @pl.loop(1, sections)
+    def _(step):
+        pl.semaphore_signal(
+            barrier,
+            inc=1,
+            device_id=(lax.rem(here + step, sections), member),
+            device_id_type=MESH,
+        )
+
+    @pl.loop(1, members)
+    def _(step):
+        pl.semaphore_signal(
+            barrier, inc=1, device_id=(here, lax.rem(member + step, members)), device_id_type=MESH
+        )
+
+    pl.semaphore_wait(barrier, sections - 1 + members - 1)
+
+    def columns(idx):
+        return pl.ds(pl.multiple_of(idx * rows, rows), rows)
+
+    def to_sibling(b):
+        return remote(sib_out.at[b], sib_in.at[b], sib_send.at[b], sib_recv.at[b], here, sibling)
+
+    def low_to_sibling(b, target):
+        return remote(
+            sibx_out.at[target, b],
+            sibx_in.at[target, b],
+            sibx_send.at[target, b],
+            sibx_recv.at[target, b],
+            here,
+            sibling,
+        )
+
+    def to_section(b, source, target):
+        return remote(
+            sibx_in.at[target, b],
+            x_in.at[source - 1, b],
+            x_send.at[target, b],
+            x_recv.at[source - 1, b],
+            target,
+            member,
+        )
+
+    def hop(b, part, side):
+        cols = last if part else wide
+        return remote(
+            z_out.at[b, :, cols],
+            z_in.at[side, b, :, cols],
+            z_send.at[part, b],
+            z_recv.at[part, side, b],
+            here,
+            member - 2 if side else member + 2,
+        )
+
+    def gain_to(other):
+        return remote(
+            gains.at[member], gains.at[member], g_send.at[other], g_recv.at[member], here, other
+        )
+
+    def gain_from(other):
+        return remote(
+            gains.at[other], gains.at[other], g_send.at[other], g_recv.at[other], here, other
+        )
+
+    def for_lower(idx, target):
+        return dot(full[idx, :, wide], mixed[target]) - dot_rows(
+            x_ref[:, columns(idx)], low_rhs[target]
+        )
+
+    def far_first(act):
+        @pl.loop(0, 2 * chips)
+        def _(turn_no):
+            side = turn_no % 2
+            away = turn_no // 2
+            b = jnp.where(side == 1, away, chips - 1 - away)
+            fits = jnp.where(side == 1, jnp.where(b < chip, 1, 0), jnp.where(b > chip, 1, 0))
+
+            @pl.when(fits == 1)
+            def _():
+                act(b)
+
+        act(chip)
+
+    def for_sibling(b):
+        idx = b * 2 + 1 - core
+
+        @pl.loop(0, here)
+        def _(target):
+            sibx_out[target, b] = for_lower(idx, target).astype(BF16)
+            low_to_sibling(b, target).start()
+
+        sib_out[b, :, wide] = dot_rows(x_ref[:, columns(idx)], own_rhs[...]).astype(BF16)
+        sib_out[b, :, last] = dot_rows(up_ref[:, columns(idx)], att[...]).astype(BF16)
+        to_sibling(b).start()
+
+    def for_sections(b):
+        @pl.loop(0, here)
+        def _(target):
+            mine = for_lower(b * 2 + core, target)
+            low_to_sibling(b, target).wait_recv()
+            both = mine + sibx_in[target, b].astype(F32)
+            sibx_in[target, b] = both.astype(BF16)
+            to_section(b, here, target).start()
+
+    def along(b, part):
+        cols = last if part else wide
+
+        @pl.when(jnp.logical_and(b >= chip, chip > 0))
+        def _():
+            hop(b, part, 0).wait_recv()
+            acc[:, cols] += z_in[0, b, :, cols].astype(F32)
+
+        @pl.when(jnp.logical_and(b <= chip, chip < chips - 1))
+        def _():
+            hop(b, part, 1).wait_recv()
+            acc[:, cols] += z_in[1, b, :, cols].astype(F32)
+
+        @pl.when(b != chip)
+        def _():
+            z_out[b, :, cols] = acc[:, cols].astype(BF16)
+
+        @pl.when(b > chip)
+        def _():
+            hop(b, part, 0).start()
+
+        @pl.when(b < chip)
+        def _():
+            hop(b, part, 1).start()
+
+    def first_part(b):
+        mine = dot_rows(x_ref[:, columns(b * 2 + core)], own_rhs[...])
+        to_sibling(b).wait_recv()
+        acc[:, wide] = mine + sib_in[b, :, wide].astype(F32)
+        along(b, 0)
+
+    def second_part(b):
+        acc[:, last] = dot_rows(up_ref[:, columns(b * 2 + core)], att[...]) + sib_in[
+            b, :, last
+        ].astype(F32)
+
+        @pl.loop(here + 1, sections)
+        def _(source):
+            to_section(b, source, here).wait_recv()
+            acc[:, last] += x_in[source - 1, b].astype(F32)
+
+        along(b, 1)
+
+    far_first(for_sibling)
+    far_first(for_sections)
+    far_first(first_part)
+
+    raw = acc[:, wide]
+    out[:, wide] = raw * gain_ref[...]
+    gain_rows = jnp.sum(raw * w_ref[:, wide].astype(F32), axis=1, keepdims=True)
+    gains[member] = jnp.transpose(jnp.broadcast_to(gain_rows, (rows, 128)))[:8]
+
+    @pl.loop(1, members)
+    def _(step):
+        gain_to(lax.rem(member + step, members)).start()
+
+    far_first(second_part)
+    out[:, last] = acc[:, last]
+
+    @pl.loop(0, chips)
+    def _(b):
+        to_sibling(b).wait_send()
+
+        @pl.loop(0, here)
+        def _(target):
+            low_to_sibling(b, target).wait_send()
+            to_section(b, here, target).wait_send()
+
+        @pl.when(b != chip)
+        def _():
+            hop(b, 0, 0).wait_send()
+            hop(b, 1, 0).wait_send()
+
+    @pl.loop(1, members)
+    def _(step):
+        other = lax.rem(member + step, members)
+        gain_from(other).wait_recv()
+        gain_to(other).wait_send()
+
+
+def scattered(sections, members, x, up, full, own_rhs, low_rhs, mixed, att, w_own, gain_col):
+    rows, cols = w_own.shape
+    head = cols // 4
+    chips = members // 2
+    lower = sections - 1
+    vmem = pl.BlockSpec(memory_space=pltpu.VMEM)
+    dma = pltpu.SemaphoreType.DMA
+    return pl.pallas_call(
+        functools.partial(scatter_kernel, sections, chips),
+        out_shape=(
+            jax.ShapeDtypeStruct((rows, cols), F32),
+            jax.ShapeDtypeStruct((members, 8, rows), F32),
+        ),
+        in_specs=[vmem] * 9,
+        out_specs=(vmem,) * 2,
+        scratch_shapes=[
+            pltpu.VMEM((rows, cols), F32),
+            pltpu.VMEM((chips, rows, cols), BF16),
+            pltpu.VMEM((chips, rows, cols), BF16),
+            pltpu.VMEM((lower, chips, rows, head), BF16),
+            pltpu.VMEM((lower, chips, rows, head), BF16),
+            pltpu.VMEM((lower, chips, rows, head), BF16),
+            pltpu.VMEM((chips, rows, cols), BF16),
+            pltpu.VMEM((2, chips, rows, cols), BF16),
+            dma((chips,)),
+            dma((chips,)),
+            dma((lower, chips)),
+            dma((lower, chips)),
+            dma((lower, chips)),
+            dma((lower, chips)),
+            dma((2, chips)),
+            dma((2, 2, chips)),
+            dma((members,)),
+            dma((members,)),
+        ],
+        compiler_params=pltpu.CompilerParams(
+            collective_id=1, has_side_effects=True, vmem_limit_bytes=VMEM_BYTES
+        ),
+        cost_estimate=pl.CostEstimate(
+            flops=2 * x.size * cols, bytes_accessed=1 << 23, transcendentals=0
+        ),
+    )(x, up, full, own_rhs, low_rhs, mixed, att, w_own, gain_col)
+
+
 def on_device(inputs, upstream, weights, gain):
     sections = lax.axis_size("section")
     here = lax.axis_index("section")
@@ -280,7 +554,6 @@
     full, products, through, cross = gathered(
         sections, members, jnp.concatenate([w_scaled, w_back_own], axis=1), x, up
     )
-    wg = full.reshape(width, 4 * head)[:, : 3 * head]
     xfloat = x.astype(F32)
     inv = lax.rsqrt(jnp.mean(xfloat * xfloat, axis=1, keepdims=True) + 1e-05)
     proj = products[:, : 3 * head] * inv
@@ -342,30 +615,25 @@
     att_below = jnp.where(below, att_all, jnp.zeros((), BF16))
     scaled_proj = (grad_proj.astype(F32) * inv).astype(BF16)
     scaled_att = (att_below.astype(F32) * (inv * inv * shift)).astype(BF16)
-    by_x = dot_rows(x, jnp.concatenate([scaled_proj, scaled_att], axis=1))
     mixed = dot_rows(scaled_proj, att_below).astype(BF16)
-    term = jnp.concatenate(
-        [
-            by_x[:, : 3 * head],
-            dot_rows(up, attended),
-            dot(wg, mixed) - by_x[:, 3 * head :],
-        ],
-        axis=1,
-    ).astype(BF16)
-    total = lax.psum_scatter(term, "fsdp", scatter_dimension=0, tiled=True)
-    rows = total.shape[0]
-    handed = total[:, 4 * head :].reshape(rows, lower, head)
-    handed = jnp.concatenate([handed, jnp.zeros((rows, 1, head), BF16)], axis=1)
-    handed = lax.psum_scatter(
-        jnp.transpose(handed, (1, 0, 2)), "section", scatter_dimension=0, tiled=False
+
+    def by_layer(value):
+        return jnp.transpose(value.reshape(value.shape[0], lower, head), (1, 0, 2))
+
+    shard, gains = scattered(
+        sections,
+        members,
+        x,
+        up,
+        full,
+        scaled_proj,
+        by_layer(scaled_att),
+        by_layer(mixed),
+        attended,
+        weights[0],
+        gain_own,
     )
-    raw = total[:, : 3 * head].astype(F32)
-    shard = jnp.concatenate(
-        [raw * gain_own, total[:, 3 * head : 4 * head].astype(F32) + handed.astype(F32)], axis=1
-    )
-    gain_rows = jnp.sum(raw * w_own[:, : 3 * head], axis=1)
-    gain_sum = lax.all_gather(gain_rows, "fsdp", axis=0, tiled=True)
-    return (shard[None], gain_sum[None])
+    return (shard[None], gains[:, 0, :].reshape(1, width))
 
 
 def solution(mesh):

time: 254 us -> 177 us (0.70)
  waiting for transfers between devices: 105 us -> 10 us
  Pallas kernels: 50.6 us -> 121 us
  between operations: 14.8 us -> 1.17 us
  matrix products: 18.4 us -> 5.71 us
  blocking collectives: 22.9 us -> 12.1 us
  other arithmetic: 18.5 us -> 9.67 us
  local copies, waits for them, and re-layouts: 15.7 us -> 8.13 us
  starting transfers between devices: 5.96 us -> 8.68 us
    reduce_scatter x1 -> x0, waiting for transfers between devices: 78.2 us -> none  [on_device(): total = lax.psum_scatter(term, 'fsdp', scatter_dimension=0, tiled=True)]
    pallas_call x0 -> x1, Pallas kernels: none -> 70.1 us  [scattered(): pl.pallas_call(functools.partial(scatter_kernel, sections, chips), out_sh...]
    all_gather x1 -> x0, blocking collectives: 12.7 us -> none  [on_device(): gain_sum = lax.all_gather(gain_rows, 'fsdp', axis=0, tiled=True)]
    unnamed x3 -> x0, waiting for transfers between devices: 11.1 us -> none
    dot_general x9 -> x8, matrix products: 10.4 us -> 2.06 us  [dot(): return jnp.dot(left, right, preferred_element_type=F32)]
    concatenate x1 -> x0, other arithmetic: 5.69 us -> none  [on_device(): jnp.concatenate([by_x[:, :3 * head], dot_rows(up, attended), dot(wg, mixe...]
    ppermute x3, waiting for transfers between devices: 15.6 us -> 10 us  [on_device(): lax.ppermute(sent.astype(BF16), 'section', [(s, s - 1) for s in range(1,...]
    unnamed x53 -> x11, local copies, waits for them, and re-layouts: 6.42 us -> 2.28 us
  transfers between devices with their start and end apart: 5 -> 3, of which waited for: 4 -> 2; matrix products, arithmetic and copies ran while one was open for 3% -> 1% of each run, Pallas kernels for 0% -> 0%
where the time goes in v3:
time: 177 us; the launch traced here: 176 us
  Pallas kernels  121 us (68%)
  blocking collectives  12.1 us (7%)
  waiting for transfers between devices  10 us (6%)
  other arithmetic  9.67 us (5%)
  starting transfers between devices  8.68 us (5%)
  local copies, waits for them, and re-layouts  8.13 us (5%)
  matrix products  5.71 us (3%)
    pallas_call x1, Pallas kernels, scattered(): pl.pallas_call(functools.partial(scatter_kernel, sections, chips), out_sh...  70.1 us
    pallas_call x1, Pallas kernels, gathered(): pl.pallas_call(functools.partial(gather_kernel, sections, chips), out_sha...  50.6 us
    all_gather x1, blocking collectives, on_device(): att_all = lax.all_gather(attended, 'section', axis=0)[:lower]  12.1 us
    ppermute x3, waiting for transfers between devices, on_device(): lax.ppermute(sent.astype(BF16), 'section', [(s, s - 1) for s in range(1,...  10 us
    ppermute x3, starting transfers between devices, on_device(): lax.ppermute(sent.astype(BF16), 'section', [(s, s - 1) for s in range(1,...  8.68 us
  transfers between devices with their start and end apart: 3, of which 2 were waited for; matrix products, arithmetic and copies ran while one was open for 1% of the time, Pallas kernels for 0%

profile of v3, /device:TPU:2, one launch (start us, length us, event | category | flops | bytes accessed | tf_op | source)
XLA Modules:
  0.0 176.1 jit_solution(1745639698064576553)
XLA Ops:
  0.7 0.9 slice.127
  1.6 0.7 convert_bitcast_fusion.1
  2.3 1.1 multiply_convert_fusion
  3.4 2.1 %multiply_reduce_fusion = f32[8,32]{1,0:T(8,128)S(1)} fusion(bf16[1,8,32,4096]{3,2,1,0:T(8,128)(2,1)} %param.4), kind=kLoop, calls=%fused_computation | loop fusion | flops 3145472 | bytes 2098176 | tf_op jit(solution)/shard_map/reduce_sum | solution.py:558
  5.6 0.8 pad_maximum_fusion.w_ref
  6.4 50.6 %shard_map.59 = (bf16[8,512,512]{2,1,0:T(8,128)(2,1)}, f32[256,512]{1,0:T(8,128)}, f32[3,256,128]{2,1,0:T(8,128)}, f32[3,384,128]{2,1,0:T(8,128)}) custom-call(bf16[512,512]{1,0:T(8,128)(2,1)} %pad_maximum_fusion.w_ref, bf16[256,4096]{1,0:T(8,128)(2,1)} %bitcast.145, bf16[256,4096]{1,0:T(8,128)(2,1)} %bitcast.147), custom_call_target="tpu_custom_call" | custom-call | flops 1073741824 | bytes 8388608 | tf_op jit(solution)/shard_map/pallas_call | solution.py:234
  57.0 1.2 slice_multiply_fusion
  58.2 0.1 fusion.46
  58.5 0.1 fusion.37
  58.7 0.2 fusion.55
  58.9 0.2 fusion.17
  59.1 1.1 multiply_reduce_fusion.7
  60.3 0.2 multiply_convert_fusion.5
  60.4 0.2 fusion.61
  60.7 0.2 fusion.62
  60.9 0.2 copy.42
  61.1 0.2 copy.43
  61.3 0.2 copy.44
  61.5 0.2 convolution_convert_fusion.5
  61.8 0.1 fusion.54
  61.9 0.1 fusion.19
  62.0 0.2 multiply_reduce_fusion.3
  62.2 0.3 fusion.3
  62.5 1.9 %collective-permute-start = (bf16[256,384]{1,0:T(8,128)(2,1)S(1)}, bf16[256,384]{1,0:T(8,128)(2,1)S(1)}, u32[]{:S(2)}, u32[]{:S(2)}) collective-permute-start(bf16[256,384]{1,0:T(8,128)(2,1)S(1)} %fusion.3), channel_id=1, source_target_pairs={{8,0},{16,8},{24,16},{9,1},{17,9},{25,17},{10,2},{18,10},{26,18},{... | collective-permute-start | bytes 589832 | tf_op jit(solution)/shard_map/ppermute | solution.py:610
  64.5 0.2 convolution_convert_fusion.1.att
  64.7 12.1 %all-gather = bf16[1024,128]{1,0:T(8,128)(2,1)S(1)} all-gather(bf16[256,128]{1,0:T(8,128)(2,1)S(1)} %convolution_convert_fusion.1.att), channel_id=2, replica_groups=mesh['section'=4,'fsdp'=8] {'section'}, dimensions={0}, use_global_device_ids=true | all-gather | bytes 327680 | tf_op jit(solution)/shard_map/all_gather | solution.py:578
  76.8 0.1 copy.66
  77.0 0.9 copy.68.gain_ref
  77.9 0.2 convolution_convert_fusion.4
  78.0 0.2 multiply_reduce_fusion.6
  78.3 0.2 multiply_convert_fusion.4
  78.5 0.2 fusion.63
  78.7 0.2 fusion.64
  79.1 0.2 fusion.23
  79.2 0.2 multiply_reduce_fusion.2
  79.4 0.3 add_convert_fusion.1
  79.8 3.6 %collective-permute-start.1 = (bf16[256,384]{1,0:T(8,128)(2,1)S(1)}, bf16[256,384]{1,0:T(8,128)(2,1)S(1)}, u32[]{:S(2)}, u32[]{:S(2)}) collective-permute-start(bf16[256,384]{1,0:T(8,128)(2,1)S(1)} %add_convert_fusion.1), channel_id=1, source_target_pairs={{8,0},{16,8},{24,16},{9,1},{17,9},{25,17},{10,2},{18,10},{26,18},{... | collective-permute-start | bytes 589832 | tf_op jit(solution)/shard_map/ppermute | solution.py:610
  83.5 4.8 %collective-permute-done.1 = bf16[256,384]{1,0:T(8,128)(2,1)S(1)} collective-permute-done((bf16[256,384]{1,0:T(8,128)(2,1)S(1)}, bf16[256,384]{1,0:T(8,128)(2,1)S(1)}, u32[]{:S(2)}, u32[]{:S(2)}) %collective-permute-start.1) | collective-permute-done | bytes 196640 | tf_op jit(solution)/shard_map/ppermute | solution.py:610
  88.3 0.2 convolution_convert_fusion.3
  88.4 0.2 multiply_reduce_fusion.5
  88.7 0.2 multiply_convert_fusion.3
  88.9 0.2 fusion.65
  89.1 0.2 fusion.66
  89.4 0.1 fusion.50
  89.5 0.2 fusion.27
  89.6 0.2 multiply_reduce_fusion.1
  89.8 0.3 add_convert_fusion
  90.2 3.1 %collective-permute-start.2 = (bf16[256,384]{1,0:T(8,128)(2,1)S(1)}, bf16[256,384]{1,0:T(8,128)(2,1)S(1)}, u32[]{:S(2)}, u32[]{:S(2)}) collective-permute-start(bf16[256,384]{1,0:T(8,128)(2,1)S(1)} %add_convert_fusion), channel_id=1, source_target_pairs={{8,0},{16,8},{24,16},{9,1},{17,9},{25,17},{10,2},{18,10},{26,18},{... | collective-permute-start | bytes 589832 | tf_op jit(solution)/shard_map/ppermute | solution.py:610
  93.3 0.1 bitcast_select_fusion
  93.4 5.2 %collective-permute-done.2 = bf16[256,384]{1,0:T(8,128)(2,1)S(1)} collective-permute-done((bf16[256,384]{1,0:T(8,128)(2,1)S(1)}, bf16[256,384]{1,0:T(8,128)(2,1)S(1)}, u32[]{:S(2)}, u32[]{:S(2)}) %collective-permute-start.2) | collective-permute-done | bytes 196640 | tf_op jit(solution)/shard_map/ppermute | solution.py:610
  98.7 0.2 convolution_convert_fusion.2
  98.8 0.2 multiply_reduce_fusion.4
  99.1 0.2 multiply_convert_fusion.2
  99.3 0.2 fusion.67
  99.5 0.2 fusion.68
  99.8 0.1 fusion.48
  99.9 0.2 fusion.31
  100.0 0.2 fusion.6
  100.3 0.3 convolution_convert_fusion
  100.5 0.9 copy.67
  101.4 0.8 multiply_convert_fusion.1.low_rhs
  102.2 70.1 %shard_map.60 = (f32[512,512]{1,0:T(8,128)}, f32[8,8,512]{2,1,0:T(8,128)}) custom-call(bf16[256,4096]{1,0:T(8,128)(2,1)} %bitcast.146, bf16[256,4096]{1,0:T(8,128)(2,1)} %bitcast.148, bf16[8,512,512]{2,1,0:T(8,128)(2,1)} %get-tuple-element.8.full, bf16[256,384]{1,0:T(8,128)(2,1)} %copy-done.1, bf16[3,256,128]{2,1,0:T(8,128)(2,1)} %multiply_convert_fusion.1.low_rhs, ...), custom_call_target="tpu_custom_call" | custom-call | flops 1073741824 | bytes 8388608 | tf_op jit(solution)/shard_map/pallas_call | solution.py:502
  172.3 1.5 slice.124
  173.8 2.3 %copy.82 = f32[1,512,512]{2,1,0:T(8,128)} copy(f32[1,512,512]{2,1,0:T(8,128)} %bitcast.157) | data formatting | bytes 2097152
  (34 shorter events, 0.9 us)
Async XLA Ops:
  57.0 3.8 %copy-start.3 = (f32[3,384,128]{2,1,0:T(8,128)S(1)}, f32[3,384,128]{2,1,0:T(8,128)}, u32[]{:S(2)}) copy-start(f32[3,384,128]{2,1,0:T(8,128)} %get-tuple-element.10) | copy-start | bytes 1769476
  57.0 4.1 %copy-start.4 = (f32[3,256,128]{2,1,0:T(8,128)S(1)}, f32[3,256,128]{2,1,0:T(8,128)}, u32[]{:S(2)}) copy-start(f32[3,256,128]{2,1,0:T(8,128)} %get-tuple-element.11) | copy-start | bytes 1179652
  58.5 2.9 %copy-start = (f32[256,512]{1,0:T(8,128)S(1)}, f32[256,512]{1,0:T(8,128)}, u32[]{:S(2)}) copy-start(f32[256,512]{1,0:T(8,128)} %get-tuple-element.9) | copy-start | bytes 1572868
  62.5 15.3 %collective-permute-start = (bf16[256,384]{1,0:T(8,128)(2,1)S(1)}, bf16[256,384]{1,0:T(8,128)(2,1)S(1)}, u32[]{:S(2)}, u32[]{:S(2)}) collective-permute-start(bf16[256,384]{1,0:T(8,128)(2,1)S(1)} %fusion.3), channel_id=1, source_target_pairs={{8,0},{16,8},{24,16},{9,1},{17,9},{25,17},{10,2},{18,10},{26,18},{... | collective-permute-start | bytes 589832 | tf_op jit(solution)/shard_map/ppermute | solution.py:610
  64.7 15.1 %copy-start.2 = (bf16[256,128]{1,0:T(8,128)(2,1)}, bf16[256,128]{1,0:T(8,128)(2,1)S(1)}, u32[]{:S(2)}) copy-start(bf16[256,128]{1,0:T(8,128)(2,1)S(1)} %convolution_convert_fusion.1.att) | copy-start | bytes 196612
  79.8 8.5 %collective-permute-start.1 = (bf16[256,384]{1,0:T(8,128)(2,1)S(1)}, bf16[256,384]{1,0:T(8,128)(2,1)S(1)}, u32[]{:S(2)}, u32[]{:S(2)}) collective-permute-start(bf16[256,384]{1,0:T(8,128)(2,1)S(1)} %add_convert_fusion.1), channel_id=1, source_target_pairs={{8,0},{16,8},{24,16},{9,1},{17,9},{25,17},{10,2},{18,10},{26,18},{... | collective-permute-start | bytes 589832 | tf_op jit(solution)/shard_map/ppermute | solution.py:610
  90.2 8.5 %collective-permute-start.2 = (bf16[256,384]{1,0:T(8,128)(2,1)S(1)}, bf16[256,384]{1,0:T(8,128)(2,1)S(1)}, u32[]{:S(2)}, u32[]{:S(2)}) collective-permute-start(bf16[256,384]{1,0:T(8,128)(2,1)S(1)} %add_convert_fusion), channel_id=1, source_target_pairs={{8,0},{16,8},{24,16},{9,1},{17,9},{25,17},{10,2},{18,10},{26,18},{... | collective-permute-start | bytes 589832 | tf_op jit(solution)/shard_map/ppermute | solution.py:610
  100.3 2.0 %copy-start.1 = (bf16[256,384]{1,0:T(8,128)(2,1)}, bf16[256,384]{1,0:T(8,128)(2,1)S(1)}, u32[]{:S(2)}) copy-start(bf16[256,384]{1,0:T(8,128)(2,1)S(1)} %get-tuple-element.23.own_rhs) | copy-start | bytes 589828

commit v4 on v3

--- a/solution.py
+++ b/solution.py
@@ -23,9 +23,7 @@
 
 
 def turn(rows, cos_full, sin_full):
-    half = rows.shape[-1] // 2
-    swapped = jnp.concatenate([rows[:, half:], rows[:, :half]], axis=-1)
-    return rows * cos_full + swapped * sin_full
+    return rows * cos_full + pltpu.roll(rows, rows.shape[-1] // 2, 1) * sin_full
 
 
 def dot(left, right):
@@ -83,11 +81,22 @@
     w_ref,
     x_ref,
     up_ref,
+    cos_ref,
+    sin_ref,
+    keep_ref,
     full,
+    own_rhs,
+    low_rhs,
+    mixed,
+    att,
     proj,
+    squares,
     through,
     cross,
     back,
+    att_in,
+    c_out,
+    c_in,
     z_recv,
     z_right,
     z_left,
@@ -97,6 +106,10 @@
     x_send,
     sibx_recv,
     sibx_send,
+    att_send,
+    att_recv,
+    c_send,
+    c_recv,
 ):
     here = lax.axis_index("section")
     member = lax.axis_index("fsdp")
@@ -107,6 +120,7 @@
     head = w_ref.shape[1] // 4
     full[member] = w_ref[...]
     proj[...] = jnp.zeros_like(proj)
+    squares[...] = jnp.zeros_like(squares)
     through[...] = jnp.zeros_like(through)
     cross[...] = jnp.zeros_like(cross)
     greet(sections, chips, here, chip, core)
@@ -143,6 +157,8 @@
         return pl.ds(pl.multiple_of(idx * rows, rows), rows)
 
     def products(idx):
+        wide = x_ref[:, columns(idx)].astype(F32)
+        squares[...] += jnp.sum(wide * wide, axis=1, keepdims=True)
         proj[:, : 3 * head] += dot(x_ref[:, columns(idx)], full[idx, :, : 3 * head])
         proj[:, 3 * head :] += dot(up_ref[:, columns(idx)], full[idx, :, 3 * head :])
 
@@ -220,10 +236,90 @@
             fits = jnp.logical_and(b >= 0, b < chips)
             pl.when(jnp.logical_and(fits, away >= first))(functools.partial(act, b))
 
+    def att_to(source, section):
+        return remote(
+            att, att_in.at[source], att_send.at[section], att_recv.at[source], section, member
+        )
+
+    def term_to(source, target):
+        return remote(
+            c_out.at[target],
+            c_in.at[source - 1],
+            c_send.at[target],
+            c_recv.at[source - 1],
+            target,
+            member,
+        )
+
+    inv = lax.rsqrt(squares[...] / x_ref.shape[1] + 1e-05)
+    cos_full, sin_full, keep = cos_ref[...], sin_ref[...], keep_ref[...]
+    scale = head ** (-0.5)
+    proj[:, : 3 * head] = proj[:, : 3 * head] * inv
+    query = turn(proj[:, :head], cos_full, sin_full).astype(BF16)
+    keys = turn(proj[:, head : 2 * head], cos_full, sin_full).astype(BF16)
+    values = proj[:, 2 * head : 3 * head].astype(BF16)
+    scores = dot_cols(query, keys) * scale * keep + (keep - 1.0) * 1e30
+    expd = jnp.exp(scores - jnp.max(scores, axis=1, keepdims=True)) * keep
+    probs = expd / jnp.sum(expd, axis=1, keepdims=True)
+    probs_b = probs.astype(BF16)
+    att[...] = dot(probs_b, values).astype(BF16)
+
+    @pl.loop(here + 1, sections)
+    def _(section):
+        att_to(here, section).start()
+
+    @pl.loop(here + 1, sections)
+    def _(source):
+        term_to(source, here).wait_recv()
+        proj[:, 3 * head :] += c_in[source - 1].astype(F32)
+
+    grad_att = proj[:, 3 * head :].astype(BF16)
+    grad_probs = dot_cols(grad_att, values)
+    grad_scores = (
+        probs * (grad_probs - jnp.sum(grad_probs * probs, axis=1, keepdims=True)) * scale
+    ).astype(BF16)
+    grad_proj = jnp.concatenate(
+        [
+            turn(dot(grad_scores, keys), cos_full, -sin_full),
+            turn(dot_rows(grad_scores, query), cos_full, -sin_full),
+            dot_rows(probs_b, grad_att),
+        ],
+        axis=1,
+    ).astype(BF16)
+    grad_wide = grad_proj.astype(F32)
+    shift = jnp.sum(grad_wide * proj[:, : 3 * head], axis=1, keepdims=True) / x_ref.shape[1]
+    own_rhs[...] = (grad_wide * inv).astype(BF16)
+    part = inv * inv * shift
+
+    @pl.loop(0, here)
+    def _(step):
+        target = here - 1 - step
+        term = inv * dot(grad_proj, cross[target].astype(BF16)) - part * through[target]
+        c_out[target] = term.astype(BF16)
+        term_to(here, target).start()
+
+    low_rhs[...] = jnp.zeros_like(low_rhs)
+    mixed[...] = jnp.zeros_like(mixed)
+
+    @pl.loop(0, here)
+    def _(source):
+        att_to(source, here).wait_recv()
+        low = att_in[source]
+        low_rhs[source] = (low.astype(F32) * part).astype(BF16)
+        mixed[source] = dot_rows(own_rhs[...], low).astype(BF16)
+
     pl.loop(0, chips)(done)
 
-
-def gathered(sections, members, w_rows, x, up):
+    @pl.loop(here + 1, sections)
+    def _(section):
+        att_to(here, section).wait_send()
+
+    @pl.loop(0, here)
+    def _(target):
+        term_to(here, target).wait_send()
+
+
+def gathered(sections, members, w_rows, x, up, cos_full, sin_full, keep):
     rows, cols = w_rows.shape
     head = cols // 4
     tokens = x.shape[0]
@@ -235,14 +331,22 @@
         functools.partial(gather_kernel, sections, chips),
         out_shape=(
             jax.ShapeDtypeStruct((members, rows, cols), BF16),
-            jax.ShapeDtypeStruct((tokens, cols), F32),
-            jax.ShapeDtypeStruct((lower, tokens, head), F32),
-            jax.ShapeDtypeStruct((lower, 3 * head, head), F32),
+            jax.ShapeDtypeStruct((tokens, 3 * head), BF16),
+            jax.ShapeDtypeStruct((lower, tokens, head), BF16),
+            jax.ShapeDtypeStruct((lower, 3 * head, head), BF16),
+            jax.ShapeDtypeStruct((tokens, head), BF16),
         ),
-        in_specs=[vmem] * 3,
-        out_specs=(vmem,) * 4,
+        in_specs=[vmem] * 6,
+        out_specs=(vmem,) * 5,
         scratch_shapes=[
+            pltpu.VMEM((tokens, cols), F32),
+            pltpu.VMEM((tokens, 1), F32),
+            pltpu.VMEM((lower, tokens, head), F32),
+            pltpu.VMEM((lower, 3 * head, head), F32),
             pltpu.VMEM((lower, members, rows, head), BF16),
+            pltpu.VMEM((lower, tokens, head), BF16),
+            pltpu.VMEM((lower, tokens, head), BF16),
+            pltpu.VMEM((lower, tokens, head), BF16),
             dma((chips,)),
             dma((chips,)),
             dma((chips,)),
@@ -252,6 +356,10 @@
             dma((sections, chips)),
             dma((lower, chips)),
             dma((lower, chips)),
+            dma((sections,)),
+            dma((lower,)),
+            dma((lower,)),
+            dma((lower,)),
         ],
         compiler_params=pltpu.CompilerParams(
             collective_id=0, has_side_effects=True, vmem_limit_bytes=VMEM_BYTES
@@ -259,7 +367,7 @@
         cost_estimate=pl.CostEstimate(
             flops=2 * tokens * members * rows * cols, bytes_accessed=1 << 23, transcendentals=0
         ),
-    )(w_rows, x, up)
+    )(w_rows, x, up, cos_full, sin_full, keep)
 
 
 def scatter_kernel(
@@ -538,11 +646,9 @@
 
 def on_device(inputs, upstream, weights, gain):
     sections = lax.axis_size("section")
-    here = lax.axis_index("section")
     micro_count, length, width = inputs.shape[1:]
     head = weights.shape[2] // 4
     tokens = micro_count * length
-    lower = sections - 1
     x = inputs[0].reshape(tokens, width)
     up = upstream.reshape(tokens, width)
     w_own = weights[0].astype(F32)
@@ -551,85 +657,32 @@
     w_back_own = weights[0][:, 3 * head :]
 
     members = lax.axis_size("fsdp")
-    full, products, through, cross = gathered(
-        sections, members, jnp.concatenate([w_scaled, w_back_own], axis=1), x, up
-    )
-    xfloat = x.astype(F32)
-    inv = lax.rsqrt(jnp.mean(xfloat * xfloat, axis=1, keepdims=True) + 1e-05)
-    proj = products[:, : 3 * head] * inv
-    direct = products[:, 3 * head :]
-
     cosine, sine = rope_tables(length, head)
     cos_full = jnp.tile(jnp.concatenate([cosine, cosine], axis=1), (micro_count, 1))
     sin_full = jnp.tile(jnp.concatenate([-sine, sine], axis=1), (micro_count, 1))
-    query = turn(proj[:, :head], cos_full, sin_full).astype(BF16)
-    keys = turn(proj[:, head : 2 * head], cos_full, sin_full).astype(BF16)
-    values = proj[:, 2 * head :].astype(BF16)
-    scale = head ** (-0.5)
     row = lax.broadcasted_iota(jnp.int32, (tokens, tokens), 0)
     col = lax.broadcasted_iota(jnp.int32, (tokens, tokens), 1)
-    seen = jnp.logical_and(row // length == col // length, row >= col)
-    scores = jnp.where(seen, dot_cols(query, keys) * scale, -1e30)
-    peak = jnp.max(scores, axis=1, keepdims=True)
-    expd = jnp.where(seen, jnp.exp(scores - peak), 0.0)
-    probs = expd / jnp.sum(expd, axis=1, keepdims=True)
-    probs_b = probs.astype(BF16)
-    attended = dot(probs_b, values).astype(BF16)
-    att_all = lax.all_gather(attended, "section", axis=0)[:lower]
-    att_all = jnp.transpose(att_all, (1, 0, 2)).reshape(tokens, lower * head)
-
-    cross = jnp.transpose(cross, (1, 0, 2)).reshape(3 * head, lower * head).astype(BF16)
-    through = jnp.transpose(through, (1, 0, 2)).reshape(tokens, lower * head) * inv
-
-    def backward(grad_att):
-        grad_att = grad_att.astype(BF16)
-        grad_probs = dot_cols(grad_att, values)
-        grad_scores = (
-            probs
-            * (grad_probs - jnp.sum(grad_probs * probs, axis=1, keepdims=True))
-            * scale
-        ).astype(BF16)
-        return jnp.concatenate(
-            [
-                turn(dot(grad_scores, keys), cos_full, -sin_full),
-                turn(dot_rows(grad_scores, query), cos_full, -sin_full),
-                dot_rows(probs_b, grad_att),
-            ],
-            axis=1,
-        ).astype(BF16)
-
-    received = jnp.zeros((tokens, lower * head), BF16)
-    own_at = jnp.minimum(here, lower - 1) * head
-    for tick in range(sections):
-        own = lax.dynamic_slice_in_dim(received, own_at, head, 1).astype(F32)
-        own = jnp.where(here == sections - 1, 0.0, own)
-        grad_proj = backward(direct + own)
-        shift = jnp.sum(grad_proj.astype(F32) * proj, axis=1, keepdims=True) / width
-        if tick < sections - 1:
-            sent = received.astype(F32) + inv * (dot(grad_proj, cross) - shift * through)
-            received = lax.ppermute(
-                sent.astype(BF16), "section", [(s, s - 1) for s in range(1, sections)]
-            )
-
-    below = lax.iota(jnp.int32, lower * head)[None, :] < here * head
-    att_below = jnp.where(below, att_all, jnp.zeros((), BF16))
-    scaled_proj = (grad_proj.astype(F32) * inv).astype(BF16)
-    scaled_att = (att_below.astype(F32) * (inv * inv * shift)).astype(BF16)
-    mixed = dot_rows(scaled_proj, att_below).astype(BF16)
-
-    def by_layer(value):
-        return jnp.transpose(value.reshape(value.shape[0], lower, head), (1, 0, 2))
-
+    keep = jnp.logical_and(row // length == col // length, row >= col).astype(F32)
+    full, own_rhs, low_rhs, mixed, att = gathered(
+        sections,
+        members,
+        jnp.concatenate([w_scaled, w_back_own], axis=1),
+        x,
+        up,
+        cos_full,
+        sin_full,
+        keep,
+    )
     shard, gains = scattered(
         sections,
         members,
         x,
         up,
         full,
-        scaled_proj,
-        by_layer(scaled_att),
-        by_layer(mixed),
-        attended,
+        own_rhs,
+        low_rhs,
+        mixed,
+        att,
         weights[0],
         gain_own,
     )

time: 177 us -> 151 us (0.85)
  Pallas kernels: 121 us -> 140 us
  blocking collectives: 12.1 us -> 0 us
  waiting for transfers between devices: 10 us -> 0 us
  starting transfers between devices: 8.68 us -> 0 us
  other arithmetic: 9.67 us -> 3.71 us
  matrix products: 5.71 us -> 0 us
    pallas_call x1, Pallas kernels: 50.6 us -> 66.9 us  [gathered(): pl.pallas_call(functools.partial(gather_kernel, sections, chips), out_sha...]
    all_gather x1 -> x0, blocking collectives: 12.1 us -> none  [on_device(): att_all = lax.all_gather(attended, 'section', axis=0)[:lower]]
    ppermute x3 -> x0, waiting for transfers between devices: 10 us -> none  [on_device(): lax.ppermute(sent.astype(BF16), 'section', [(s, s - 1) for s in range(1,...]
    ppermute x3 -> x0, starting transfers between devices: 8.68 us -> none  [on_device(): lax.ppermute(sent.astype(BF16), 'section', [(s, s - 1) for s in range(1,...]
    dot_general x22 -> x0, matrix products: 5.71 us -> none  [the longest x8 2.06 us: dot(): return jnp.dot(left, right, preferred_element_type=F32)]
    reduce_sum x6 -> x0, other arithmetic: 3.1 us -> none  [the longest x1 2.08 us: on_device(): inv = lax.rsqrt(jnp.mean(xfloat * xfloat, axis=1, keepdims=True) + 1e-05)]
    pallas_call x1, Pallas kernels: 70.1 us -> 72.8 us  [scattered(): pl.pallas_call(functools.partial(scatter_kernel, sections, chips), out_sh...]
  transfers between devices with their start and end apart: 3 -> 0, of which waited for: 2 -> 0; matrix products, arithmetic and copies ran while one was open for 1% -> 0% of each run, Pallas kernels for 0% -> 0%
where the time goes in v4:
time: 151 us
  Pallas kernels  140 us (93%)
  local copies, waits for them, and re-layouts  6.88 us (5%)
  other arithmetic  3.71 us (2%)
    pallas_call x1, Pallas kernels, scattered(): pl.pallas_call(functools.partial(scatter_kernel, sections, chips), out_sh...  72.8 us
    pallas_call x1, Pallas kernels, gathered(): pl.pallas_call(functools.partial(gather_kernel, sections, chips), out_sha...  66.9 us

profile of v4, /device:TPU:2, one launch (start us, length us, event | category | flops | bytes accessed | tf_op | source)
XLA Modules:
  0.0 151.0 jit_solution(15539674435191181172)
XLA Ops:
  0.7 0.7 convert_bitcast_fusion
  1.4 0.1 fusion.4
  1.4 0.1 pad_maximum_fusion.1
  1.5 0.7 tile.8
  2.2 0.7 tile.20
  2.9 0.9 slice.17
  3.8 0.9 fusion.1.keep_ref
  4.6 0.9 copy.6.gain_ref
  5.5 1.1 multiply_convert_fusion
  6.6 0.8 pad_maximum_fusion.w_ref
  7.5 66.9 %shard_map.59 = (bf16[8,512,512]{2,1,0:T(8,128)(2,1)}, bf16[256,384]{1,0:T(8,128)(2,1)}, bf16[3,256,128]{2,1,0:T(8,128)(2,1)}, bf16[3,384,128]{2,1,0:T(8,128)(2,1)}, bf16[256,128]{1,0:T(8,128)(2,1)}) custom-call(bf16[512,512]{1,0:T(8,128)(2,1)} %pad_maximum_fusion.w_ref, bf16[256,4096]{1,0:T(8,128)(2,1)} %bitcast.10, bf16[256,4096]{1,0:T(8,128)(2,1)} %bitcast.12, ...), custom_call_target="tpu_custom_call" | custom-call | flops 1073741824 | bytes 8388608 | tf_op jit(solution)/shard_map/pallas_call | solution.py:330
  74.4 72.8 %shard_map.60 = (f32[512,512]{1,0:T(8,128)}, f32[8,8,512]{2,1,0:T(8,128)}) custom-call(bf16[256,4096]{1,0:T(8,128)(2,1)} %bitcast.11, bf16[256,4096]{1,0:T(8,128)(2,1)} %bitcast.13, bf16[8,512,512]{2,1,0:T(8,128)(2,1)} %get-tuple-element.9.full, bf16[256,384]{1,0:T(8,128)(2,1)} %get-tuple-element.10.own_rhs, bf16[3,256,128]{2,1,0:T(8,128)(2,1)} %get-tuple-element.11.low_rhs, ...), custom_call_target="tpu_custom_call" | custom-call | flops 1073741824 | bytes 8388608 | tf_op jit(solution)/shard_map/pallas_call | solution.py:610
  147.2 1.5 %slice.15 = f32[8,1,512]{2,1,0:T(1,128)} slice(f32[8,8,512]{2,1,0:T(8,128)} %get-tuple-element.15), slice={[0:8], [0:1], [0:512]} | slice | bytes 32768 | tf_op jit(solution)/shard_map/slice | solution.py:689
  148.8 2.3 %copy.8 = f32[1,512,512]{2,1,0:T(8,128)} copy(f32[1,512,512]{2,1,0:T(8,128)} %bitcast.17) | data formatting | bytes 2097152
  (3 shorter events, 0.0 us)

commit v5 on v4

v5 whole, which is shorter than its diff:
```python
import functools

import jax
import jax.numpy as jnp
import numpy as np
from jax import lax
from jax.experimental import pallas as pl
from jax.experimental.pallas import tpu as pltpu
from jax.sharding import PartitionSpec as P

MESH = pl.DeviceIdType.MESH
VMEM_BYTES = 56 * 1024 * 1024

F32 = jnp.float32
BF16 = jnp.bfloat16


def tables(micro_count, length, head):
    freq = 500000.0 ** (-2.0 * np.arange(head // 2) / head)
    angle = np.arange(length)[:, None] * freq[None, :]
    cosine, sine = np.cos(angle), np.sin(angle)
    cos_full = np.tile(np.concatenate([cosine, cosine], axis=1), (micro_count, 1))
    sin_full = np.tile(np.concatenate([-sine, sine], axis=1), (micro_count, 1))
    token = np.arange(micro_count * length)
    same = token[:, None] // length == token[None, :] // length
    keep = np.logical_and(same, token[:, None] >= token[None, :])
    return tuple(jnp.asarray(table.astype(np.float32)) for table in (cos_full, sin_full, keep))


def turn(rows, cos_full, sin_full):
    return rows * cos_full + pltpu.roll(rows, rows.shape[-1] // 2, 1) * sin_full


def dot(left, right):
    return jnp.dot(left, right, preferred_element_type=F32)


def dot_rows(left, right):
    return lax.dot_general(left, right, (((0,), (0,)), ((), ())), preferred_element_type=F32)


def dot_cols(left, right):
    return lax.dot_general(left, right, (((1,), (1,)), ((), ())), preferred_element_type=F32)


def remote(src, dst, send_sem, recv_sem, section, member):
    return pltpu.make_async_remote_copy(
        src_ref=src,
        dst_ref=dst,
        send_sem=send_sem,
        recv_sem=recv_sem,
        device_id=(section, member),
        device_id_type=MESH,
    )


def layer_kernel(
    sections,
    chips,
    w_ref,
    gain_ref,
    x_ref,
    up_ref,
    cos_ref,
    sin_ref,
    keep_ref,
    out,
    gain_out,
    full,
    gain_col,
    own_rhs,
    low_rhs,
    mixed,
    att,
    proj,
    squares,
    through,
    cross,
    back,
    att_in,
    c_out,
    c_in,
    acc,
    sib_out,
    sib_in,
    x_in,
    z_out,
    z_in,
    gains,
    ready,
    z_recv,
    z_right,
    z_left,
    sib_recv,
    sib_send,
    x_recv,
    x_send,
    sibx_recv,
    sibx_send,
    att_send,
    att_recv,
    c_send,
    c_recv,
    sum_send,
    sum_recv,
    low_send,
    low_recv,
    e_send,
    e_recv,
    zs_send,
    zs_recv,
    g_send,
    g_recv,
):
    here = lax.axis_index("section")
    member = lax.axis_index("fsdp")
    members = 2 * chips
    chip = member // 2
    core = member % 2
    sibling = chip * 2 + 1 - core
    rows = w_ref.shape[0]
    head = w_ref.shape[1] // 4
    wide = pl.ds(0, 3 * head)
    last = pl.ds(3 * head, head)
    gain_col[...] = jnp.transpose(jnp.broadcast_to(gain_ref[...].astype(F32), (128, rows)))
    full[member, :, wide] = (w_ref[:, wide].astype(F32) * gain_col[:, :1]).astype(BF16)
    full[member, :, last] = w_ref[:, last]
    proj[...] = jnp.zeros_like(proj)
    squares[...] = jnp.zeros_like(squares)
    through[...] = jnp.zeros_like(through)
    cross[...] = jnp.zeros_like(cross)

    barrier = pltpu.get_barrier_semaphore()

    @pl.loop(1, sections)
    def _(step):
        pl.semaphore_signal(
            barrier,
            inc=1,
            device_id=(lax.rem(here + step, sections), member),
            device_id_type=MESH,
        )

    @pl.loop(1, members)
    def _(step):
        pl.semaphore_signal(
            barrier, inc=1, device_id=(here, lax.rem(member + step, members)), device_id_type=MESH
        )

    pl.semaphore_wait(barrier, sections - 1 + members - 1)

    def to_right(b):
        block = full.at[b * 2 + core]
        return remote(block, block, z_right.at[b], z_recv.at[b], here, member + 2)

    def to_left(b):
        block = full.at[b * 2 + core]
        return remote(block, block, z_left.at[b], z_recv.at[b], here, member - 2)

    def to_sibling(b, lane):
        block = full.at[b * 2 + lane]
        return remote(block, block, sib_send.at[b], sib_recv.at[b], here, sibling)

    def to_section(b, source, section):
        return remote(
            full.at[b * 2 + core, :, pl.ds(3 * head, head)],
            back.at[source, b * 2 + core],
            x_send.at[section, b],
            x_recv.at[source, b],
            section,
            member,
        )

    def back_to_sibling(b, source, lane):
        block = back.at[source, b * 2 + lane]
        return remote(
            block, block, sibx_send.at[source, b], sibx_recv.at[source, b], here, sibling
        )

    def columns(idx):
        return pl.ds(pl.multiple_of(idx * rows, rows), rows)

    def products(idx):
        part_x = x_ref[:, columns(idx)].astype(F32)
        squares[...] += jnp.sum(part_x * part_x, axis=1, keepdims=True)
        proj[:, : 3 * head] += dot(x_ref[:, columns(idx)], full[idx, :, : 3 * head])
        proj[:, 3 * head :] += dot(up_ref[:, columns(idx)], full[idx, :, 3 * head :])

    def back_products(source, idx):
        through[source] += dot(x_ref[:, columns(idx)], back[source, idx])
        cross[source] += dot_rows(full[idx, :, : 3 * head], back[source, idx])

    def arrived(b):
        @pl.when(b < chip)
        def _():
            to_right(b).wait_recv()

        @pl.when(b > chip)
        def _():
            to_left(b).wait_recv()

        @pl.when(jnp.logical_and(b <= chip, chip < chips - 1))
        def _():
            to_right(b).start()

        @pl.when(jnp.logical_and(b >= chip, chip > 0))
        def _():
            to_left(b).start()

        to_sibling(b, core).start()

        @pl.loop(here + 1, sections)
        def _(section):
            to_section(b, here, section).start()

        products(b * 2 + core)

    def second(b):
        to_sibling(b, 1 - core).wait_recv()
        products(b * 2 + 1 - core)

        @pl.loop(0, here)
        def _(source):
            to_section(b, source, here).wait_recv()
            back_to_sibling(b, source, core).start()
            back_products(source, b * 2 + core)

    def third(b):
        @pl.loop(0, here)
        def _(source):
            back_to_sibling(b, source, 1 - core).wait_recv()
            back_products(source, b * 2 + 1 - core)

    def done(b):
        @pl.when(jnp.logical_and(b <= chip, chip < chips - 1))
        def _():
            to_right(b).wait_send()

        @pl.when(jnp.logical_and(b >= chip, chip > 0))
        def _():
            to_left(b).wait_send()

        to_sibling(b, core).wait_send()

        @pl.loop(here + 1, sections)
        def _(section):
            to_section(b, here, section).wait_send()

        @pl.loop(0, here)
        def _(source):
            back_to_sibling(b, source, core).wait_send()

    @pl.loop(0, 2 * (chips + 2))
    def _(turn_no):
        side = turn_no % 2
        for lag, act in enumerate((arrived, second, third)):
            away = turn_no // 2 - lag
            b = jnp.where(side == 1, chip + away, chip - away)
            first = jnp.where(side == 1, 1, 0)
            fits = jnp.logical_and(b >= 0, b < chips)
            pl.when(jnp.logical_and(fits, away >= first))(functools.partial(act, b))

    def att_to(source, section):
        return remote(
            att, att_in.at[source], att_send.at[section], att_recv.at[source], section, member
        )

    def term_to(source, target):
        return remote(
            c_out.at[target],
            c_in.at[source - 1],
            c_send.at[target],
            c_recv.at[source - 1],
            target,
            member,
        )

    inv = lax.rsqrt(squares[...] / x_ref.shape[1] + 1e-05)
    cos_full, sin_full, keep = cos_ref[...], sin_ref[...], keep_ref[...]
    scale = head ** (-0.5)
    proj[:, : 3 * head] = proj[:, : 3 * head] * inv
    query = turn(proj[:, :head], cos_full, sin_full).astype(BF16)
    keys = turn(proj[:, head : 2 * head], cos_full, sin_full).astype(BF16)
    values = proj[:, 2 * head : 3 * head].astype(BF16)
    scores = dot_cols(query, keys) * scale * keep + (keep - 1.0) * 1e30
    expd = jnp.exp(scores - jnp.max(scores, axis=1, keepdims=True)) * keep
    probs = expd / jnp.sum(expd, axis=1, keepdims=True)
    probs_b = probs.astype(BF16)
    att[...] = dot(probs_b, values).astype(BF16)

    @pl.loop(here + 1, sections)
    def _(section):
        att_to(here, section).start()

    @pl.loop(here + 1, sections)
    def _(source):
        term_to(source, here).wait_recv()
        proj[:, 3 * head :] += c_in[source - 1].astype(F32)

    grad_att = proj[:, 3 * head :].astype(BF16)
    grad_probs = dot_cols(grad_att, values)
    grad_scores = (
        probs * (grad_probs - jnp.sum(grad_probs * probs, axis=1, keepdims=True)) * scale
    ).astype(BF16)
    grad_proj = jnp.concatenate(
        [
            turn(dot(grad_scores, keys), cos_full, -sin_full),
            turn(dot_rows(grad_scores, query), cos_full, -sin_full),
            dot_rows(probs_b, grad_att),
        ],
        axis=1,
    ).astype(BF16)
    grad_wide = grad_proj.astype(F32)
    shift = jnp.sum(grad_wide * proj[:, : 3 * head], axis=1, keepdims=True) / x_ref.shape[1]
    own_rhs[...] = (grad_wide * inv).astype(BF16)
    part = inv * inv * shift

    @pl.loop(0, here)
    def _(step):
        target = here - 1 - step
        term = inv * dot(grad_proj, cross[target].astype(BF16)) - part * through[target]
        c_out[target] = term.astype(BF16)
        term_to(here, target).start()

    low_rhs[...] = jnp.zeros_like(low_rhs)
    mixed[...] = jnp.zeros_like(mixed)

    @pl.loop(0, here)
    def _(source):
        att_to(source, here).wait_recv()
        low = att_in[source]
        low_rhs[source] = (low.astype(F32) * part).astype(BF16)
        mixed[source] = dot_rows(own_rhs[...], low).astype(BF16)

    pl.loop(0, chips)(done)

    @pl.loop(here + 1, sections)
    def _(section):
        att_to(here, section).wait_send()

    @pl.loop(0, here)
    def _(target):
        term_to(here, target).wait_send()

    def sum_to_sibling(b):
        return remote(sib_out.at[b], sib_in.at[b], sum_send.at[b], sum_recv.at[b], here, sibling)

    def low_to_sibling(b, target):
        return remote(
            back.at[target, 2 * b],
            back.at[target, 2 * b + 1],
            low_send.at[target, b],
            low_recv.at[target, b],
            here,
            sibling,
        )

    def low_to_section(b, source, target):
        return remote(
            back.at[target, 2 * b + 1],
            x_in.at[source - 1, b],
            e_send.at[target, b],
            e_recv.at[source - 1, b],
            target,
            member,
        )

    def hop(b, part, side):
        cols = last if part else wide
        return remote(
            z_out.at[b, :, cols],
            z_in.at[side, b, :, cols],
            zs_send.at[part, b],
            zs_recv.at[part, side, b],
            here,
            member - 2 if side else member + 2,
        )

    def gain_to(other):
        return remote(
            gains.at[:, columns(member)], gains.at[:, columns(member)], g_send.at[other], g_recv.at[member], here, other
        )

    def gain_from(other):
        return remote(
            gains.at[:, columns(other)], gains.at[:, columns(other)], g_send.at[other], g_recv.at[other], here, other
        )

    def for_lower(idx, target):
        return dot(full[idx, :, wide], mixed[target]) - dot_rows(
            x_ref[:, columns(idx)], low_rhs[target]
        )

    def far_first(act):
        @pl.loop(0, 2 * chips)
        def _(turn_no):
            side = turn_no % 2
            away = turn_no // 2
            b = jnp.where(side == 1, away, chips - 1 - away)
            fits = jnp.where(side == 1, jnp.where(b < chip, 1, 0), jnp.where(b > chip, 1, 0))

            @pl.when(fits == 1)
            def _():
                act(b)

        act(chip)

    def low_for_sibling(b):
        @pl.loop(0, here)
        def _(target):
            back[target, 2 * b] = for_lower(b * 2 + 1 - core, target).astype(BF16)
            low_to_sibling(b, target).start()

    def for_sibling(b):
        idx = b * 2 + 1 - core
        sib_out[b, :, wide] = dot_rows(x_ref[:, columns(idx)], own_rhs[...]).astype(BF16)
        sib_out[b, :, last] = dot_rows(up_ref[:, columns(idx)], att[...]).astype(BF16)
        sum_to_sibling(b).start()

    def for_sections(b):
        @pl.loop(0, here)
        def _(target):
            mine = for_lower(b * 2 + core, target)
            low_to_sibling(b, target).wait_recv()
            both = mine + back[target, 2 * b + 1].astype(F32)
            back[target, 2 * b + 1] = both.astype(BF16)
            low_to_section(b, here, target).start()

    def along(b, part):
        cols = last if part else wide

        @pl.when(jnp.logical_and(b >= chip, chip > 0))
        def _():
            hop(b, part, 0).wait_recv()
            acc[:, cols] += z_in[0, b, :, cols].astype(F32)

        @pl.when(jnp.logical_and(b <= chip, chip < chips - 1))
        def _():
            hop(b, part, 1).wait_recv()
            acc[:, cols] += z_in[1, b, :, cols].astype(F32)

        @pl.when(b != chip)
        def _():
            z_out[b, :, cols] = acc[:, cols].astype(BF16)

        @pl.when(b > chip)
        def _():
            hop(b, part, 0).start()

        @pl.when(b < chip)
        def _():
            hop(b, part, 1).start()

    def first_part(b):
        mine = dot_rows(x_ref[:, columns(b * 2 + core)], own_rhs[...])
        sum_to_sibling(b).wait_recv()
        acc[:, wide] = mine + sib_in[b, :, wide].astype(F32)
        along(b, 0)

    def second_part(b):
        acc[:, last] = dot_rows(up_ref[:, columns(b * 2 + core)], att[...]) + sib_in[
            b, :, last
        ].astype(F32)

        @pl.loop(here + 1, sections)
        def _(source):
            low_to_section(b, source, here).wait_recv()
            acc[:, last] += x_in[source - 1, b].astype(F32)

        along(b, 1)

    pl.semaphore_signal(ready, inc=1, device_id=(here, sibling), device_id_type=MESH)
    far_first(for_sibling)
    pl.semaphore_wait(ready, 1)
    far_first(low_for_sibling)
    far_first(for_sections)
    far_first(first_part)

    raw = acc[:, wide]
    out[:, wide] = raw * gain_col[:, :1]
    gain_rows = jnp.sum(raw * w_ref[:, wide].astype(F32), axis=1, keepdims=True)
    gains[:, columns(member)] = jnp.transpose(jnp.broadcast_to(gain_rows, (rows, 128)))[:8]

    @pl.loop(1, members)
    def _(step):
        gain_to(lax.rem(member + step, members)).start()

    far_first(second_part)
    out[:, last] = acc[:, last]

    @pl.loop(0, chips)
    def _(b):
        sum_to_sibling(b).wait_send()

        @pl.loop(0, here)
        def _(target):
            low_to_sibling(b, target).wait_send()
            low_to_section(b, here, target).wait_send()

        @pl.when(b != chip)
        def _():
            hop(b, 0, 0).wait_send()
            hop(b, 1, 0).wait_send()

    @pl.loop(1, members)
    def _(step):
        other = lax.rem(member + step, members)
        gain_from(other).wait_recv()
        gain_to(other).wait_send()
    gain_out[...] = gains[:1]


def layer(sections, members, w_own, gain_row, x, up, cos_full, sin_full, keep):
    rows, cols = w_own.shape
    head = cols // 4
    tokens = x.shape[0]
    chips = members // 2
    lower = sections - 1
    vmem = pl.BlockSpec(memory_space=pltpu.VMEM)
    dma = pltpu.SemaphoreType.DMA
    return pl.pallas_call(
        functools.partial(layer_kernel, sections, chips),
        out_shape=(
            jax.ShapeDtypeStruct((rows, cols), F32),
            jax.ShapeDtypeStruct((1, members * rows), F32),
        ),
        in_specs=[vmem] * 7,
        out_specs=(vmem,) * 2,
        scratch_shapes=[
            pltpu.VMEM((members, rows, cols), BF16),
            pltpu.VMEM((rows, 128), F32),
            pltpu.VMEM((tokens, 3 * head), BF16),
            pltpu.VMEM((lower, tokens, head), BF16),
            pltpu.VMEM((lower, 3 * head, head), BF16),
            pltpu.VMEM((tokens, head), BF16),
            pltpu.VMEM((tokens, cols), F32),
            pltpu.VMEM((tokens, 1), F32),
            pltpu.VMEM((lower, tokens, head), F32),
            pltpu.VMEM((lower, 3 * head, head), F32),
            pltpu.VMEM((lower, members, rows, head), BF16),
            pltpu.VMEM((lower, tokens, head), BF16),
            pltpu.VMEM((lower, tokens, head), BF16),
            pltpu.VMEM((lower, tokens, head), BF16),
            pltpu.VMEM((rows, cols), F32),
            pltpu.VMEM((chips, rows, cols), BF16),
            pltpu.VMEM((chips, rows, cols), BF16),
            pltpu.VMEM((lower, chips, rows, head), BF16),
            pltpu.VMEM((chips, rows, cols), BF16),
            pltpu.VMEM((2, chips, rows, cols), BF16),
            pltpu.VMEM((8, members * rows), F32),
            pltpu.SemaphoreType.REGULAR,
            dma((chips,)),
            dma((chips,)),
            dma((chips,)),
            dma((chips,)),
            dma((chips,)),
            dma((lower, chips)),
            dma((sections, chips)),
            dma((lower, chips)),
            dma((lower, chips)),
            dma((sections,)),
            dma((lower,)),
            dma((lower,)),
            dma((lower,)),
            dma((chips,)),
            dma((chips,)),
            dma((lower, chips)),
            dma((lower, chips)),
            dma((lower, chips)),
            dma((lower, chips)),
            dma((2, chips)),
            dma((2, 2, chips)),
            dma((members,)),
            dma((members,)),
        ],
        compiler_params=pltpu.CompilerParams(
            collective_id=0, has_side_effects=True, vmem_limit_bytes=VMEM_BYTES
        ),
        cost_estimate=pl.CostEstimate(
            flops=6 * x.size * cols, bytes_accessed=1 << 23, transcendentals=0
        ),
    )(w_own, gain_row, x, up, cos_full, sin_full, keep)


def on_device(inputs, upstream, weights, gain):
    micro_count, length, width = inputs.shape[1:]
    head = weights.shape[2] // 4
    tokens = micro_count * length
    cos_full, sin_full, keep = tables(micro_count, length, head)
    shard, gain_sum = layer(
        lax.axis_size("section"),
        lax.axis_size("fsdp"),
        weights[0],
        gain,
        inputs[0].reshape(tokens, width),
        upstream.reshape(tokens, width),
        cos_full,
        sin_full,
        keep,
    )
    return (shard[None], gain_sum)


def solution(mesh):
    return jax.shard_map(
        on_device,
        mesh=mesh,
        in_specs=(
            P("section", None, "fsdp", None),
            P(None, "fsdp", None),
            P("section", "fsdp", None),
            P("section", "fsdp"),
        ),
        out_specs=(P("section", "fsdp", None), P("section", None)),
        check_vma=False,
    )
```

time: 151 us -> 143 us (0.947)
  local copies, waits for them, and re-layouts: 6.88 us -> 2.88 us
  other arithmetic: 3.71 us -> 0 us
    convert_element_type x3 -> x0, other arithmetic: 2.69 us -> none  [the longest x1 1.13 us: on_device(): w_scaled = (w_own[:, :3 * head] * gain_own).astype(BF16)]
    slice x2 -> x0, local copies, waits for them, and re-layouts: 2.43 us -> none  [the longest x1 1.52 us: on_device(): return (shard[None], gains[:, 0, :].reshape(1, width))]
    pallas_call x2 -> x1, Pallas kernels: 140 us -> 140 us  [layer(): pl.pallas_call(functools.partial(layer_kernel, sections, chips), out_shap...]
where the time goes in v5:
time: 143 us
  Pallas kernels  140 us (98%)
  local copies, waits for them, and re-layouts  2.88 us (2%)
    pallas_call x1, Pallas kernels, layer(): pl.pallas_call(functools.partial(layer_kernel, sections, chips), out_shap...  140 us
    unnamed x4, local copies, waits for them, and re-layouts  2.88 us

profile of v5, /device:TPU:2, one launch (start us, length us, event | category | flops | bytes accessed | tf_op | source)
XLA Modules:
  0.0 143.1 jit_solution(13331096153865861323)
XLA Ops:
  0.6 139.6 %shard_map.86 = (f32[512,512]{1,0:T(8,128)}, f32[1,4096]{1,0:T(1,128)}) custom-call(bf16[512,512]{1,0:T(8,128)(2,1)} %bitcast.7, bf16[1,512]{1,0:T(2,128)(2,1)} %gain_ref.1, bf16[256,4096]{1,0:T(8,128)(2,1)} %bitcast.5, bf16[256,4096]{1,0:T(8,128)(2,1)} %bitcast.6, f32[256,128]{1,0:T(8,128)} %constant.6.clone.cos_ref, f32[256,128]{1,0:T(8,128)} %constant.7.clone.sin_ref, ...), custom_call_target="tpu_custom_call" | custom-call | flops 3221225472 | bytes 8388608 | tf_op jit(solution)/shard_map/pallas_call | solution.py:521
  140.2 0.0 copy-start
  140.3 2.3 %copy.11 = f32[1,512,512]{2,1,0:T(8,128)} copy(f32[1,512,512]{2,1,0:T(8,128)} %bitcast.4) | data formatting | bytes 2097152
  142.5 0.0 copy-done
  142.5 0.6 copy.12
Async XLA Ops:
  140.2 2.3 %copy-start = (f32[1,4096]{1,0:T(1,128)S(1)}, f32[1,4096]{1,0:T(1,128)}, u32[]{:S(2)}) copy-start(f32[1,4096]{1,0:T(1,128)} %get-tuple-element.9) | copy-start | bytes 49156

commit v6 on v5

--- a/solution.py
+++ b/solution.py
@@ -9,7 +9,7 @@
 from jax.sharding import PartitionSpec as P
 
 MESH = pl.DeviceIdType.MESH
-VMEM_BYTES = 56 * 1024 * 1024
+VMEM_BYTES = 62 * 1024 * 1024
 
 F32 = jnp.float32
 BF16 = jnp.bfloat16
@@ -68,6 +68,9 @@
     gain_out,
     full,
     gain_col,
+    x_turned,
+    up_turned,
+    w_turned,
     own_rhs,
     low_rhs,
     mixed,
@@ -181,6 +184,9 @@
         return pl.ds(pl.multiple_of(idx * rows, rows), rows)
 
     def products(idx):
+        x_turned[idx] = jnp.transpose(x_ref[:, columns(idx)])
+        up_turned[idx] = jnp.transpose(up_ref[:, columns(idx)])
+        w_turned[idx] = jnp.transpose(full[idx, :, : 3 * head])
         part_x = x_ref[:, columns(idx)].astype(F32)
         squares[...] += jnp.sum(part_x * part_x, axis=1, keepdims=True)
         proj[:, : 3 * head] += dot(x_ref[:, columns(idx)], full[idx, :, : 3 * head])
@@ -188,7 +194,7 @@
 
     def back_products(source, idx):
         through[source] += dot(x_ref[:, columns(idx)], back[source, idx])
-        cross[source] += dot_rows(full[idx, :, : 3 * head], back[source, idx])
+        cross[source] += dot(w_turned[idx], back[source, idx])
 
     def arrived(b):
         @pl.when(b < chip)
@@ -387,9 +393,7 @@
         )
 
     def for_lower(idx, target):
-        return dot(full[idx, :, wide], mixed[target]) - dot_rows(
-            x_ref[:, columns(idx)], low_rhs[target]
-        )
+        return dot(full[idx, :, wide], mixed[target]) - dot(x_turned[idx], low_rhs[target])
 
     def far_first(act):
         @pl.loop(0, 2 * chips)
@@ -413,8 +417,8 @@
 
     def for_sibling(b):
         idx = b * 2 + 1 - core
-        sib_out[b, :, wide] = dot_rows(x_ref[:, columns(idx)], own_rhs[...]).astype(BF16)
-        sib_out[b, :, last] = dot_rows(up_ref[:, columns(idx)], att[...]).astype(BF16)
+        sib_out[b, :, wide] = dot(x_turned[idx], own_rhs[...]).astype(BF16)
+        sib_out[b, :, last] = dot(up_turned[idx], att[...]).astype(BF16)
         sum_to_sibling(b).start()
 
     def for_sections(b):
@@ -452,13 +456,13 @@
             hop(b, part, 1).start()
 
     def first_part(b):
-        mine = dot_rows(x_ref[:, columns(b * 2 + core)], own_rhs[...])
+        mine = dot(x_turned[b * 2 + core], own_rhs[...])
         sum_to_sibling(b).wait_recv()
         acc[:, wide] = mine + sib_in[b, :, wide].astype(F32)
         along(b, 0)
 
     def second_part(b):
-        acc[:, last] = dot_rows(up_ref[:, columns(b * 2 + core)], att[...]) + sib_in[
+        acc[:, last] = dot(up_turned[b * 2 + core], att[...]) + sib_in[
             b, :, last
         ].astype(F32)
 
@@ -529,6 +533,9 @@
         scratch_shapes=[
             pltpu.VMEM((members, rows, cols), BF16),
             pltpu.VMEM((rows, 128), F32),
+            pltpu.VMEM((members, rows, tokens), BF16),
+            pltpu.VMEM((members, rows, tokens), BF16),
+            pltpu.VMEM((members, 3 * head, rows), BF16),
             pltpu.VMEM((tokens, 3 * head), BF16),
             pltpu.VMEM((lower, tokens, head), BF16),
             pltpu.VMEM((lower, 3 * head, head), BF16),

time: 143 us -> 143 us (level)
  no operation moved by 1% of the time
where the time goes in v6:
time: 143 us
  Pallas kernels  139 us (97%)
  local copies, waits for them, and re-layouts  2.88 us (2%)
    pallas_call x1, Pallas kernels, layer(): pl.pallas_call(functools.partial(layer_kernel, sections, chips), out_shap...  139 us
    unnamed x4, local copies, waits for them, and re-layouts  2.88 us

profile of v6, /device:TPU:2, one launch (start us, length us, event | category | flops | bytes accessed | tf_op | source)
XLA Modules:
  0.0 142.5 jit_solution(11826365749987821101)
XLA Ops:
  0.6 139.0 %shard_map.86 = (f32[512,512]{1,0:T(8,128)}, f32[1,4096]{1,0:T(1,128)}) custom-call(bf16[512,512]{1,0:T(8,128)(2,1)} %bitcast.7, bf16[1,512]{1,0:T(2,128)(2,1)} %gain_ref.1, bf16[256,4096]{1,0:T(8,128)(2,1)} %bitcast.5, bf16[256,4096]{1,0:T(8,128)(2,1)} %bitcast.6, f32[256,128]{1,0:T(8,128)} %constant.6.clone.cos_ref, f32[256,128]{1,0:T(8,128)} %constant.7.clone.sin_ref, ...), custom_call_target="tpu_custom_call" | custom-call | flops 3221225472 | bytes 8388608 | tf_op jit(solution)/shard_map/pallas_call | solution.py:525
  139.7 0.0 copy-start
  139.7 2.3 %copy.11 = f32[1,512,512]{2,1,0:T(8,128)} copy(f32[1,512,512]{2,1,0:T(8,128)} %bitcast.4) | data formatting | bytes 2097152
  141.9 0.0 copy-done
  141.9 0.6 copy.12
Async XLA Ops:
  139.7 2.3 %copy-start = (f32[1,4096]{1,0:T(1,128)S(1)}, f32[1,4096]{1,0:T(1,128)}, u32[]{:S(2)}) copy-start(f32[1,4096]{1,0:T(1,128)} %get-tuple-element.9) | copy-start | bytes 49156
